TPU v7x, 32 devices: a whole 2x2x4 slice. The times are simulated.
32 devices in a mesh: row: 4 (over x, core), col: 8 (over z, y).
Axes of the slice: x: 2, y: 2, z: 4, core: 2. Of those that a mesh axis runs over, the one named last changes fastest.
Arguments:
- derivs: bfloat16 [256, 65536], P(('row', 'col')), may hold values from -15 to 15, as said below
- energy_derivs: bfloat16 [256, 65536], P(('row', 'col')), may hold values from -15 to 15, as said below
- energies: float32 [256], P(('row', 'col')), may hold values from -30 to -10, as said below
Outputs:
- correlation: float32 [4096, 65536], P('row', 'col')
- hamiltonian: float32 [4096, 65536], P('row', 'col')
Inputs may be any that keep to these rules, and one draw needn't show every extreme that they name: `derivs`: finite values. `energy_derivs`: finite values. `energies`: finite values.
All inputs are finite; a program needn't handle non-finite values.
Results may differ from a plain program's by a relative error of at most 0.0041.
Values may be sent and summed in bfloat16 or wider, within the bound.
No kernel may reach another device: no remote copies, remote signals or barrier semaphores. Data moves between devices by JAX's collectives and lax.ppermute only.
A program may use at most 128 MiB of HBM per device.

v0:
```python
import jax
import jax.numpy as jnp
from jax import lax
from jax.sharding import PartitionSpec as P


def contract(row_block, other):
    return lax.dot_general(
        row_block, other, (((0,), (0,)), ((), ())), preferred_element_type=jnp.float32
    )


def centre_tiles(raw_derivs, raw_grads, sample_energy, mean_derivs, mean_grads, mean_energy):
    offsets = raw_derivs.astype(jnp.float32) - mean_derivs[None, :]
    centred = offsets.astype(jnp.bfloat16)
    shifted = (sample_energy - mean_energy)[:, None] * offsets
    energy_term = (shifted + (raw_grads.astype(jnp.float32) - mean_grads[None, :])).astype(
        jnp.bfloat16
    )
    return (centred, energy_term)


def fetch_rows(source):
    widened = lax.all_gather(source, "col", axis=0, tiled=True)
    return (lax.all_to_all(widened, "row", split_axis=1, concat_axis=0, tiled=True), "row_major")


def body(derivs, energy_derivs, energies):
    row_count = lax.axis_size("row")
    col_count = lax.axis_size("col")
    local_count = derivs.shape[0]
    total_count = local_count * row_count * col_count
    slab_width = derivs.shape[1] // 16
    every_energy = lax.all_gather(energies, ("row", "col"), axis=0, tiled=True)
    mean_energy = jnp.sum(every_energy) / total_count
    moving = (derivs, energy_derivs)
    row_source = derivs[:, :slab_width]
    row_data, row_order = fetch_rows(row_source)
    row_full = row_data.astype(jnp.float32)
    row_data = (row_full - (jnp.sum(row_full, axis=0) / total_count)[None, :]).astype(jnp.bfloat16)
    tiles = (
        lax.all_to_all(moving[0], "col", split_axis=1, concat_axis=0, tiled=True),
        lax.all_to_all(moving[1], "col", split_axis=1, concat_axis=0, tiled=True),
    )
    tile_totals = lax.psum(
        (
            jnp.sum(tiles[0].astype(jnp.float32), axis=0),
            jnp.sum(tiles[1].astype(jnp.float32), axis=0),
        ),
        "row",
    )
    group_energy = lax.dynamic_slice_in_dim(
        every_energy, lax.axis_index("row") * (col_count * local_count), col_count * local_count, 0
    )
    tiles = centre_tiles(
        tiles[0],
        tiles[1],
        group_energy,
        tile_totals[0] / total_count,
        tile_totals[1] / total_count,
        mean_energy,
    )
    correlation_sum = contract(row_data, lax.all_gather(tiles[0], "row", axis=0, tiled=True))
    hamil_sum = contract(row_data, lax.all_gather(tiles[1], "row", axis=0, tiled=True))
    return (correlation_sum / total_count, hamil_sum / total_count)


def solution(mesh):
    placed = (P(("row", "col"), None), P(("row", "col"), None), P(("row", "col")))
    return jax.shard_map(
        body,
        mesh=mesh,
        in_specs=placed,
        out_specs=(P("row", "col"), P("row", "col")),
        check_vma=False,
    )
```

profile of v0, /device:TPU:0, one launch (start us, length us, event | category | flops | bytes accessed | tf_op | source)
XLA Modules:
  0.0 220.5 jit_solution(2932104656370193316)
XLA Ops:
  7.2 0.0 copy-start
  7.2 33.1 %all_to_all.39 = bf16[8,8,8192]{2,0,1:T(8,128)(2,1)S(1)} all-to-all(bf16[8,8,8192]{2,0,1:T(8,128)(2,1)} %bitcast.40), channel_id=1, replica_groups=mesh['row'=4,'col'=8] {'col'}, dimensions={1} | all-to-all | bytes 2097152 | tf_op jit(solution)/shard_map/all_to_all | solution.py:42
  40.2 3.6 %all-to-all-start.2 = ((bf16[8,8,8192]{2,0,1:T(8,128)(2,1)}), bf16[8,8,8192]{2,0,1:T(8,128)(2,1)S(1)}, u32[]{:S(2)}, u32[]{:S(2)}) async-start(bf16[8,8,8192]{2,0,1:T(8,128)(2,1)} %bitcast.41), calls=%async_computation.2 | async-start | bytes 2097152 | tf_op jit(solution)/shard_map/all_to_all | solution.py:43
  43.8 0.0 all-reduce.4.cloned.1.call-start
  43.9 0.0 copy-done
  43.9 0.2 dynamic-update-slice
  44.1 45.3 %all-reduce = f32[256]{0:T(256)S(1)} all-reduce(f32[256]{0:T(256)S(1)} %dynamic-update-slice), channel_id=1, replica_groups=mesh['row'=4,'col'=8] {'row','col'}, use_global_device_ids=true, to_apply=%add | all-reduce | flops 256 | bytes 2048
  89.5 0.6 reduce_sum.38
  90.7 0.8 convert_reduce_fusion.1
  91.5 0.0 all-to-all-done.2
  91.5 0.8 convert_reduce_fusion
  92.3 0.0 all-reduce.4.cloned.1.call-update
  92.3 0.0 all-gather.5.cloned.1.call-start
  92.4 0.1 dynamic-slice_subtract_fusion
  92.5 31.2 %all-reduce.4.cloned.1.call-done = (f32[8192]{0:T(1024)}, f32[8192]{0:T(1024)}) async-done(((f32[8192]{0:T(1024)}, f32[8192]{0:T(1024)}), (f32[8192]{0:T(1024)}, f32[8192]{0:T(1024)})) %all-reduce.4.cloned.1.call-update) | async-done | bytes 65552 | tf_op jit(solution)/shard_map/psum | solution.py:45
  123.7 0.8 broadcast_multiply_fusion
  124.5 1.8 fusion.4
  126.3 0.0 all-gather.5.cloned.1.call-update
  126.4 0.0 all-gather.3.cloned.1.call-start
  126.4 0.7 all-gather.3.cloned.1.call-update
  127.1 0.8 slice.3
  127.9 31.4 %all_gather.12 = bf16[64,4096]{1,0:T(8,128)(2,1)S(1)} all-gather(bf16[8,4096]{1,0:T(8,128)(2,1)S(1)} %slice.3), channel_id=1, replica_groups=mesh['row'=4,'col'=8] {'col'}, dimensions={0}, use_global_device_ids=true | all-gather | bytes 589824 | tf_op jit(solution)/shard_map/all_gather | solution.py:24
  159.4 11.2 %all_to_all.40 = bf16[64,4,1024]{2,0,1:T(8,128)(2,1)S(1)} all-to-all(bf16[64,4,1024]{2,0,1:T(8,128)(2,1)S(1)} %bitcast.39), channel_id=1, replica_groups=mesh['row'=4,'col'=8] {'row'}, dimensions={1} | all-to-all | bytes 1048576 | tf_op jit(solution)/shard_map/all_to_all | solution.py:25
  170.6 0.1 convert_reduce_fusion.2
  170.7 0.1 fusion.6
  170.8 0.0 all-gather.5.cloned.1.call-done
  170.9 17.0 %convolution_multiply_fusion = f32[1024,8192]{1,0:T(8,128)} fusion(bf16[256,1024]{1,0:T(8,128)(2,1)S(1)} %fusion.6, bf16[256,8192]{1,0:T(8,128)(2,1)} %all-gather.5.cloned.1.call-done), kind=kOutput, calls=%fused_computation | convolution fusion | flops 4303355904 | bytes 38273024 | tf_op jit(solution)/shard_map/dot_general | solution.py:8
  187.9 9.9 %all-gather.3.cloned.1.call-done = bf16[256,8192]{1,0:T(8,128)(2,1)} async-done(((bf16[64,8192]{1,0:T(8,128)(2,1)}), bf16[256,8192]{1,0:T(8,128)(2,1)}) %all-gather.3.cloned.1.call-update) | async-done | bytes 4194320 | tf_op jit(solution)/shard_map/all_gather | solution.py:63
  197.7 16.2 %convolution_multiply_fusion.1 = f32[1024,8192]{1,0:T(8,128)} fusion(bf16[256,1024]{1,0:T(8,128)(2,1)S(1)} %fusion.6, bf16[256,8192]{1,0:T(8,128)(2,1)} %all-gather.3.cloned.1.call-done), kind=kOutput, calls=%fused_computation.1 | convolution fusion | flops 4303355904 | bytes 38273024 | tf_op jit(solution)/shard_map/dot_general | solution.py:8
  (3 shorter events, 0.0 us)
Async XLA Ops:
  7.2 36.7 %copy-start = (f32[8]{0:T(128)S(1)}, f32[8]{0:T(128)}, u32[]{:S(2)}) copy-start(f32[8]{0:T(128)} %param.5) | copy-start | bytes 100
  40.2 51.3 %all-to-all-start.2 = ((bf16[8,8,8192]{2,0,1:T(8,128)(2,1)}), bf16[8,8,8192]{2,0,1:T(8,128)(2,1)S(1)}, u32[]{:S(2)}, u32[]{:S(2)}) async-start(bf16[8,8,8192]{2,0,1:T(8,128)(2,1)} %bitcast.41), calls=%async_computation.2 | async-start | bytes 2097152 | tf_op jit(solution)/shard_map/all_to_all | solution.py:43
  43.8 79.9 %all-reduce.4.cloned.1.call-start = ((), (), s32[]{:S(2)}) async-start(), calls=%async_computation.5 | async-start | bytes 131072 | tf_op jit(solution)/shard_map/psum | solution.py:45
  92.3 78.5 %all-gather.5.cloned.1.call-start = ((), (), s32[]{:S(2)}) async-start(), calls=%async_computation.4 | async-start | bytes 5242880 | tf_op jit(solution)/shard_map/all_gather | solution.py:64
  126.4 71.4 %all-gather.3.cloned.1.call-start = ((), (), s32[]{:S(2)}) async-start(), calls=%async_computation.3 | async-start | bytes 5242880 | tf_op jit(solution)/shard_map/all_gather | solution.py:63
Sparse Core Ops, SparseCore 0:
  92.5 31.2 all-reduce.3
  126.5 34.4 all-gather.4
  163.2 34.4 all-gather.2
where the time goes:
time: 221 us
  blocking collectives  121 us (55%)
  waiting for transfers between devices  41.9 us (19%)
  matrix products  33.2 us (15%)
  between operations  14.5 us (7%)
  other arithmetic  5.11 us (2%)
  starting transfers between devices  3.71 us (2%)
    unnamed x1, blocking collectives  45.3 us
    dot_general x2, matrix products, contract(): lax.dot_general(row_block, other, (((0,), (0,)), ((), ())), preferred_ele...  33.2 us
    all_to_all x1, blocking collectives, body(): lax.all_to_all(moving[0], 'col', split_axis=1, concat_axis=0, tiled=True)  33.1 us
    all_gather x1, blocking collectives, fetch_rows(): widened = lax.all_gather(source, 'col', axis=0, tiled=True)  31.4 us
    psum x1, waiting for transfers between devices, body(): lax.psum((jnp.sum(tiles[0].astype(jnp.float32), axis=0), jnp.sum(tiles[1]...  31.2 us
    all_to_all x1, blocking collectives, fetch_rows(): lax.all_to_all(widened, 'row', split_axis=1, concat_axis=0, tiled=True)  11.2 us
    all_gather x1, waiting for transfers between devices, body(): lax.all_gather(tiles[0], 'row', axis=0, tiled=True)  9.89 us
  transfers between devices with their start and end apart: 4, of which 2 were waited for; matrix products, arithmetic and copies ran while one was open for 9% of the time, Pallas kernels for 0%

commit v1 on v0

v1 whole, which is shorter than its diff:
```python
import functools
import jax
import jax.numpy as jnp
from jax import lax
from jax.experimental import pallas as pl
from jax.experimental.pallas import tpu as pltpu
from jax.sharding import PartitionSpec as P

VMEM_BYTES = 40 * 1024 * 1024
LANES = 128
SHARES = (4, 3, 1)


def averaged(values, count):
    if count & (count - 1) == 0:
        return values * (1.0 / count)
    return values / count


def prepare_kernel(first_half, second_half, energy, row_out, shift_out):
    count = energy.shape[0]
    half = first_half.shape[1]
    for place, source in enumerate((first_half, second_half)):
        raw = source[...].astype(jnp.float32)
        centred = raw - averaged(jnp.sum(raw, axis=0, keepdims=True), count)
        row_out[place * half : (place + 1) * half, :] = centred.T.astype(jnp.bfloat16)
    parts = energy[...].astype(jnp.float32)
    value = (parts[:, 0:1] + parts[:, 1:2]) + parts[:, 2:3]
    shift = value - averaged(jnp.sum(value, axis=0, keepdims=True), count)
    shift_out[...] = jnp.broadcast_to(shift, shift_out.shape)


def prepare(first_half, second_half, energy):
    count, half = first_half.shape
    return pl.pallas_call(
        prepare_kernel,
        out_shape=(
            jax.ShapeDtypeStruct((2 * half, count), jnp.bfloat16),
            jax.ShapeDtypeStruct((count, LANES), jnp.float32),
        ),
        compiler_params=pltpu.CompilerParams(vmem_limit_bytes=VMEM_BYTES),
        cost_estimate=pl.CostEstimate(flops=4 * half * count, bytes_accessed=8 * half * count, transcendentals=0),
    )(first_half, second_half, energy)


def chunk_kernel(row_ref, shift_ref, *refs, pieces):
    derivs = refs[:pieces]
    grads = refs[pieces : 2 * pieces]
    correlation, hamiltonian = refs[-2:]
    count = row_ref.shape[1]
    raw = jnp.concatenate([piece[...] for piece in derivs], axis=0).astype(jnp.float32)
    raw_grads = jnp.concatenate([piece[...] for piece in grads], axis=0).astype(jnp.float32)
    offsets = raw - averaged(jnp.sum(raw, axis=0, keepdims=True), count)
    grad_offsets = raw_grads - averaged(jnp.sum(raw_grads, axis=0, keepdims=True), count)
    centred = offsets.astype(jnp.bfloat16)
    term = (shift_ref[:, 0:1] * offsets + grad_offsets).astype(jnp.bfloat16)
    rows = row_ref[...]
    correlation[...] = averaged(jnp.dot(rows, centred, preferred_element_type=jnp.float32), count)
    hamiltonian[...] = averaged(jnp.dot(rows, term, preferred_element_type=jnp.float32), count)


def chunk_products(rows, shift, pieces, start, width, block, total_width, earlier):
    steps = width // block
    first = start // block
    n_rows = rows.shape[0]
    specs = [pl.BlockSpec(rows.shape, lambda j: (0, 0)), pl.BlockSpec(shift.shape, lambda j: (0, 0))]
    for offset in (0, steps):
        specs += [pl.BlockSpec((p.shape[0], block), lambda j, o=offset: (0, j + o)) for p in pieces]
    operands = [rows, shift, *pieces, *pieces]
    aliases = {}
    if earlier is not None:
        aliases = {len(operands): 0, len(operands) + 1: 1}
        operands += list(earlier)
        specs += [pl.BlockSpec(memory_space=pl.ANY)] * 2
    return pl.pallas_call(
        functools.partial(chunk_kernel, pieces=len(pieces)),
        grid=(steps,),
        in_specs=specs,
        out_specs=[pl.BlockSpec((n_rows, block), lambda j: (0, j + first))] * 2,
        out_shape=[jax.ShapeDtypeStruct((n_rows, total_width), jnp.float32)] * 2,
        input_output_aliases=aliases,
        compiler_params=pltpu.CompilerParams(vmem_limit_bytes=VMEM_BYTES),
        cost_estimate=pl.CostEstimate(
            flops=4 * n_rows * width * rows.shape[1], bytes_accessed=8 * n_rows * width, transcendentals=0
        ),
    )(*operands)


def energy_parts(energies):
    high = lax.reduce_precision(energies, 8, 7)
    rest = energies - high
    middle = lax.reduce_precision(rest, 8, 7)
    low = rest - middle
    parts = jnp.stack((high, middle, low), axis=1).astype(jnp.bfloat16)
    return jnp.pad(parts, ((0, 0), (0, LANES - 3)))


def across(value, axis, distance):
    size = lax.axis_size(axis)
    return lax.ppermute(value, axis, [(i, i ^ distance) for i in range(size)])


def body(derivs, energy_derivs, energies):
    row_count = lax.axis_size("row")
    col_count = lax.axis_size("col")
    local = derivs.shape[0]
    total_width = derivs.shape[1] // col_count
    slab = derivs.shape[1] // 16
    row_width = slab // row_count
    half = row_width // 2
    row = lax.axis_index("row")
    odd = lax.axis_index("col") % 2

    unit = total_width // sum(SHARES)
    widths = [unit * s for s in SHARES]
    starts = [sum(widths[:i]) for i in range(len(widths))]
    block = min(512, unit)

    tiles = (derivs.reshape(local, col_count, total_width), energy_derivs.reshape(local, col_count, total_width))

    slab_tiles = derivs[:, :slab].reshape(local, row_count // 2, 2 * row_width)
    tagged = energy_parts(energies)
    mine = lax.dynamic_index_in_dim(slab_tiles, row // 2, 1, keepdims=False)
    other = lax.dynamic_index_in_dim(slab_tiles, (row // 2) ^ 1, 1, keepdims=False)
    got = across(jnp.concatenate((other, tagged), axis=1), "row", 2)
    pair = (jnp.concatenate((mine, tagged), axis=1), got)

    def for_core(block_pair, core):
        return [
            jnp.concatenate(
                (lax.dynamic_slice_in_dim(b, core * row_width, row_width, 1), b[:, 2 * row_width :]), axis=1
            )
            for b in block_pair
        ]

    own_parts = for_core(pair, row % 2)
    sent = jnp.concatenate(for_core(pair, 1 - row % 2), axis=1)
    got = across(sent, "row", 1)
    piece_width = row_width + LANES
    slab_parts = own_parts + [got[:, :piece_width], got[:, piece_width:]]
    halves = [
        jnp.concatenate([jnp.concatenate((p[:, h * half : (h + 1) * half], p[:, row_width:]), axis=1) for p in slab_parts], axis=1)
        for h in range(2)
    ]
    slab_send = jnp.stack([halves[q % 2] for q in range(col_count)], axis=1)

    outs = None
    rows = shift = None
    gathered = []
    for i, (start, width) in enumerate(zip(starts, widths)):
        parts = [t[:, :, start : start + width] for t in tiles]
        if i == 1:
            parts.append(slab_send)
        swapped = lax.all_to_all(jnp.concatenate(parts, axis=2), "col", split_axis=1, concat_axis=0, tiled=True)
        swapped = swapped.reshape(local * col_count, swapped.shape[2])
        if i == 1:
            slab_got = swapped[:, 2 * width :]
            swapped = swapped[:, : 2 * width]
            tail = half + LANES
            held = jnp.concatenate([slab_got[:, q * tail : (q + 1) * tail] for q in range(4)], axis=0)
            energy = held[:, half:]
            held = held[:, :half]
            fetched = across(held, "col", 1)
            rows, shift = prepare(
                jnp.where(odd == 0, held, fetched), jnp.where(odd == 0, fetched, held), energy
            )
        far = across(swapped, "row", 2)
        gathered.append((swapped, far, across(swapped, "row", 1), across(far, "row", 1)))
    for start, width, pieces in zip(starts, widths, gathered):
        outs = chunk_products(rows, shift, pieces, start, width, block, total_width, outs)
    return tuple(outs)


def solution(mesh):
    placed = (P(("row", "col"), None), P(("row", "col"), None), P(("row", "col")))
    return jax.shard_map(
        body,
        mesh=mesh,
        in_specs=placed,
        out_specs=(P("row", "col"), P("row", "col")),
        check_vma=False,
    )
```

time: 221 us -> 129 us (0.58)
  blocking collectives: 121 us -> 0 us
  matrix products: 33.2 us -> 0 us
  Pallas kernels: 0 us -> 27.6 us
  waiting for transfers between devices: 41.9 us -> 63.5 us
  starting transfers between devices: 3.71 us -> 23.6 us
  between operations: 14.5 us -> 0.96 us
  local copies, waits for them, and re-layouts: 1.13 us -> 6.13 us
    all_to_all x1 -> x3, waiting for transfers between devices: 0.01 us -> 49.1 us  [body(): lax.all_to_all(jnp.concatenate(parts, axis=2), 'col', split_axis=1, conca...]
    unnamed x1 -> x0, blocking collectives: 45.3 us -> none
    all_to_all x2 -> x0, blocking collectives: 44.3 us -> none  [the longest x1 33.1 us: body(): lax.all_to_all(moving[0], 'col', split_axis=1, concat_axis=0, tiled=True)]
    dot_general x2 -> x0, matrix products: 33.2 us -> none  [contract(): lax.dot_general(row_block, other, (((0,), (0,)), ((), ())), preferred_ele...]
    all_gather x1 -> x0, blocking collectives: 31.4 us -> none  [fetch_rows(): widened = lax.all_gather(source, 'col', axis=0, tiled=True)]
    psum x1 -> x0, waiting for transfers between devices: 31.2 us -> none  [body(): lax.psum((jnp.sum(tiles[0].astype(jnp.float32), axis=0), jnp.sum(tiles[1]...]
    pallas_call x0 -> x4, Pallas kernels: none -> 27.6 us  [the longest x3 27.1 us: chunk_products(): pl.pallas_call(functools.partial(chunk_kernel, pieces=len(pieces)), grid=...]
    ppermute x0 -> x12, waiting for transfers between devices: none -> 14.4 us  [across(): return lax.ppermute(value, axis, [(i, i ^ distance) for i in range(size)])]
  transfers between devices with their start and end apart: 4 -> 15, of which waited for: 2 -> 4; matrix products, arithmetic and copies ran while one was open for 9% -> 8% of each run, Pallas kernels for 0% -> 18%
where the time goes in v1:
time: 129 us; the launch traced here: 127 us
  waiting for transfers between devices  63.5 us (49%)
  Pallas kernels  27.6 us (21%)
  starting transfers between devices  23.6 us (18%)
  local copies, waits for them, and re-layouts  6.13 us (5%)
  other arithmetic  5.41 us (4%)
    all_to_all x3, waiting for transfers between devices, body(): lax.all_to_all(jnp.concatenate(parts, axis=2), 'col', split_axis=1, conca...  49.1 us
    pallas_call x3, Pallas kernels, chunk_products(): pl.pallas_call(functools.partial(chunk_kernel, pieces=len(pieces)), grid=...  27.1 us
    ppermute x12, waiting for transfers between devices, across(): return lax.ppermute(value, axis, [(i, i ^ distance) for i in range(size)])  14.4 us
    all_to_all x3, starting transfers between devices, body(): lax.all_to_all(jnp.concatenate(parts, axis=2), 'col', split_axis=1, conca...  13.3 us
    ppermute x12, starting transfers between devices, across(): return lax.ppermute(value, axis, [(i, i ^ distance) for i in range(size)])  10.3 us
    slice x6, local copies, waits for them, and re-layouts, body(): parts = [t[:, :, start:start + width] for t in tiles]  4.14 us
    concatenate x3, other arithmetic, body(): jnp.concatenate(parts, axis=2)  2.84 us
  transfers between devices with their start and end apart: 15, of which 4 were waited for; matrix products, arithmetic and copies ran while one was open for 8% of the time, Pallas kernels for 18%

profile of v1, /device:TPU:0, one launch (start us, length us, event | category | flops | bytes accessed | tf_op | source)
XLA Modules:
  0.0 127.2 jit_solution(9922396857550282986)
XLA Ops:
  0.7 0.8 slice.94
  1.5 0.7 fusion.2
  2.2 0.1 copy.14
  2.3 3.0 %collective-permute-start = (bf16[8,2176]{1,0:T(8,128)(2,1)S(1)}, bf16[8,2176]{1,0:T(8,128)(2,1)S(1)}, u32[]{:S(2)}, u32[]{:S(2)}) collective-permute-start(bf16[8,2176]{1,0:T(8,128)(2,1)S(1)} %pad_maximum_fusion.5), channel_id=1, source_target_pairs={{0,16},{8,24},{16,0},{24,8},{1,17},{9,25},{17,1},{25,9},{2,18},{10... | collective-permute-start | bytes 104456 | tf_op jit(solution)/shard_map/ppermute | solution.py:100
  5.4 1.1 slice.134
  6.4 1.1 slice.135
  7.6 0.1 collective-permute-start.1
  7.7 1.0 pad_maximum_fusion.1
  8.7 6.0 %all-to-all-start.2 = ((bf16[8,8,8192]{2,0,1:T(8,128)(2,1)}), bf16[8,8,8192]{2,0,1:T(8,128)(2,1)}, u32[]{:S(2)}, u32[]{:S(2)}) async-start(bf16[8,8,8192]{2,0,1:T(8,128)(2,1)} %pad_maximum_fusion.1), calls=%async_computation.2 | async-start | bytes 2097152 | tf_op jit(solution)/shard_map/all_to_all | solution.py:154
  14.8 1.0 slice.117
  16.0 1.1 pad_maximum_fusion
  17.0 24.2 %all-to-all-done.2 = bf16[8,8,8192]{2,0,1:T(8,128)(2,1)} async-done(((bf16[8,8,8192]{2,0,1:T(8,128)(2,1)}), bf16[8,8,8192]{2,0,1:T(8,128)(2,1)}, u32[]{:S(2)}, u32[]{:S(2)}) %all-to-all-start.2) | async-done | bytes 1048608 | tf_op jit(solution)/shard_map/all_to_all | solution.py:154
  41.3 3.6 %all-to-all-start = ((bf16[8,8,8704]{2,0,1:T(8,128)(2,1)}), bf16[8,8,8704]{2,0,1:T(8,128)(2,1)S(1)}, u32[]{:S(2)}, u32[]{:S(2)}) async-start(bf16[8,8,8704]{2,0,1:T(8,128)(2,1)} %pad_maximum_fusion), calls=%async_computation | async-start | bytes 2228224 | tf_op jit(solution)/shard_map/all_to_all | solution.py:154
  44.9 1.5 %collective-permute-start.9 = (bf16[64,8192]{1,0:T(8,128)(2,1)}, bf16[64,8192]{1,0:T(8,128)(2,1)}, u32[]{:S(2)}, u32[]{:S(2)}) collective-permute-start(bf16[64,8192]{1,0:T(8,128)(2,1)} %bitcast.22.refs_0_.refs_4_), channel_id=1, source_target_pairs={{0,16},{8,24},{16,0},{24,8},{1,17},{9,25},{17,1},{25,9},{2,18},{10... | collective-permute-start | bytes 3145736 | tf_op jit(solution)/shard_map/ppermute | solution.py:100
  46.4 0.9 slice.132
  47.4 0.1 collective-permute-start.10
  47.4 24.8 %all-to-all-done = bf16[8,8,8704]{2,0,1:T(8,128)(2,1)S(1)} async-done(((bf16[8,8,8704]{2,0,1:T(8,128)(2,1)}), bf16[8,8,8704]{2,0,1:T(8,128)(2,1)S(1)}, u32[]{:S(2)}, u32[]{:S(2)}) %all-to-all-start) | async-done | bytes 1114144 | tf_op jit(solution)/shard_map/all_to_all | solution.py:154
  72.3 1.6 %collective-permute-start.6 = (bf16[64,6144]{1,0:T(8,128)(2,1)S(1)}, bf16[64,6144]{1,0:T(8,128)(2,1)S(1)}, u32[]{:S(2)}, u32[]{:S(2)}) collective-permute-start(bf16[64,6144]{1,0:T(8,128)(2,1)S(1)} %slice.133.refs_0_.refs_4_), channel_id=1, source_target_pairs={{0,16},{8,24},{16,0},{24,8},{1,17},{9,25},{17,1},{25,9},{2,18},{10... | collective-permute-start | bytes 2359304 | tf_op jit(solution)/shard_map/ppermute | solution.py:100
  73.9 0.7 pad_maximum_fusion.3
  74.6 3.6 %all-to-all-start.1 = ((bf16[8,8,2048]{2,0,1:T(8,128)(2,1)}), bf16[8,8,2048]{2,0,1:T(8,128)(2,1)S(1)}, u32[]{:S(2)}, u32[]{:S(2)}) async-start(bf16[8,8,2048]{2,0,1:T(8,128)(2,1)} %pad_maximum_fusion.3), calls=%async_computation.1 | async-start | bytes 524288 | tf_op jit(solution)/shard_map/all_to_all | solution.py:154
  78.4 0.8 slice.130
  79.2 2.0 %collective-permute-start.2 = (bf16[256,512]{1,0:T(8,128)(2,1)}, bf16[256,512]{1,0:T(8,128)(2,1)}, u32[]{:S(2)}, u32[]{:S(2)}) collective-permute-start(bf16[256,512]{1,0:T(8,128)(2,1)} %slice.130), channel_id=1, source_target_pairs={{0,1},{1,0},{2,3},{3,2},{4,5},{5,4},{6,7},{7,6},{8,9},{9,8},{10,11... | collective-permute-start | bytes 786440 | tf_op jit(solution)/shard_map/ppermute | solution.py:100
  81.2 9.5 %collective-permute-done.6.refs_1_.refs_5_ = bf16[64,6144]{1,0:T(8,128)(2,1)S(1)} collective-permute-done((bf16[64,6144]{1,0:T(8,128)(2,1)S(1)}, bf16[64,6144]{1,0:T(8,128)(2,1)S(1)}, u32[]{:S(2)}, u32[]{:S(2)}) %collective-permute-start.6) | collective-permute-done | bytes 786464 | tf_op jit(solution)/shard_map/ppermute | solution.py:100
  90.8 1.6 %collective-permute-start.3 = (bf16[64,2048]{1,0:T(8,128)(2,1)S(1)}, bf16[64,2048]{1,0:T(8,128)(2,1)S(1)}, u32[]{:S(2)}, u32[]{:S(2)}) collective-permute-start(bf16[64,2048]{1,0:T(8,128)(2,1)S(1)} %bitcast.38), channel_id=1, source_target_pairs={{0,16},{8,24},{16,0},{24,8},{1,17},{9,25},{17,1},{25,9},{2,18},{10... | collective-permute-start | bytes 786440 | tf_op jit(solution)/shard_map/ppermute | solution.py:100
  92.4 0.8 pad_maximum_fusion.4.energy
  93.1 1.1 broadcast_select_fusion
  94.2 0.5 shard_map.50
  94.7 4.9 %collective-permute-done.3.refs_1_.refs_5_ = bf16[64,2048]{1,0:T(8,128)(2,1)S(1)} collective-permute-done((bf16[64,2048]{1,0:T(8,128)(2,1)S(1)}, bf16[64,2048]{1,0:T(8,128)(2,1)S(1)}, u32[]{:S(2)}, u32[]{:S(2)}) %collective-permute-start.3) | collective-permute-done | bytes 262176 | tf_op jit(solution)/shard_map/ppermute | solution.py:100
  99.5 0.5 collective-permute-start.5
  100.0 13.8 %shard_map.51 = (f32[1024,8192]{1,0:T(8,128)}, f32[1024,8192]{1,0:T(8,128)}) custom-call(bf16[1024,256]{1,0:T(8,128)(2,1)S(1)} %get-tuple-element.8.row_ref, f32[256,128]{1,0:T(8,128)S(1)} %get-tuple-element.9.shift_ref, bf16[64,8192]{1,0:T(8,128)(2,1)} %bitcast.22.refs_0_.refs_4_, bf16[64,8192]{1,0:T(8,128)(2,1)} %collective-permute-done.9.refs_1_.refs_5_, ...), custom_call_target="tpu_custom_call" | custom-call | flops 4294967296 | bytes 33554432 | tf_op jit(solution)/shard_map/pallas_call | solution.py:75
  113.8 9.3 %shard_map.52 = (f32[1024,8192]{1,0:T(8,128)}, f32[1024,8192]{1,0:T(8,128)}) custom-call(bf16[1024,256]{1,0:T(8,128)(2,1)S(1)} %get-tuple-element.8.row_ref, f32[256,128]{1,0:T(8,128)S(1)} %get-tuple-element.9.shift_ref, bf16[64,6144]{1,0:T(8,128)(2,1)S(1)} %slice.133.refs_0_.refs_4_, ...), custom_call_target="tpu_custom_call", output_to_operand_aliasing={{0}: (10, {}), {1}: (11, {})} | custom-call | flops 3221225472 | bytes 25165824 | tf_op jit(solution)/shard_map/pallas_call | solution.py:75
  123.1 4.1 %shard_map.53 = (f32[1024,8192]{1,0:T(8,128)}, f32[1024,8192]{1,0:T(8,128)}) custom-call(bf16[1024,256]{1,0:T(8,128)(2,1)S(1)} %get-tuple-element.8.row_ref, f32[256,128]{1,0:T(8,128)S(1)} %get-tuple-element.9.shift_ref, bf16[64,2048]{1,0:T(8,128)(2,1)S(1)} %bitcast.40, ...), custom_call_target="tpu_custom_call", output_to_operand_aliasing={{0}: (10, {}), {1}: (11, {})} | custom-call | flops 1073741824 | bytes 8388608 | tf_op jit(solution)/shard_map/pallas_call | solution.py:75
  (53 shorter events, 0.4 us)
Async XLA Ops:
  2.3 5.2 %collective-permute-start = (bf16[8,2176]{1,0:T(8,128)(2,1)S(1)}, bf16[8,2176]{1,0:T(8,128)(2,1)S(1)}, u32[]{:S(2)}, u32[]{:S(2)}) collective-permute-start(bf16[8,2176]{1,0:T(8,128)(2,1)S(1)} %pad_maximum_fusion.5), channel_id=1, source_target_pairs={{0,16},{8,24},{16,0},{24,8},{1,17},{9,25},{17,1},{25,9},{2,18},{10... | collective-permute-start | bytes 104456 | tf_op jit(solution)/shard_map/ppermute | solution.py:100
  7.5 7.2 %copy-start.1 = (bf16[8,65536]{1,0:T(8,128)(2,1)S(1)}, bf16[8,65536]{1,0:T(8,128)(2,1)}, u32[]{:S(2)}) copy-start(bf16[8,65536]{1,0:T(8,128)(2,1)} %param.3) | copy-start | bytes 3145732
  7.6 8.2 %collective-permute-start.1 = (bf16[8,2304]{1,0:T(8,128)(2,1)S(1)}, bf16[8,2304]{1,0:T(8,128)(2,1)S(1)}, u32[]{:S(2)}, u32[]{:S(2)}) collective-permute-start(bf16[8,2304]{1,0:T(8,128)(2,1)S(1)} %pad_maximum_fusion.6), channel_id=1, source_target_pairs={{0,8},{8,0},{16,24},{24,16},{1,9},{9,1},{17,25},{25,17},{2,10},{10... | collective-permute-start | bytes 110600 | tf_op jit(solution)/shard_map/ppermute | solution.py:100
  8.7 32.5 %all-to-all-start.2 = ((bf16[8,8,8192]{2,0,1:T(8,128)(2,1)}), bf16[8,8,8192]{2,0,1:T(8,128)(2,1)}, u32[]{:S(2)}, u32[]{:S(2)}) async-start(bf16[8,8,8192]{2,0,1:T(8,128)(2,1)} %pad_maximum_fusion.1), calls=%async_computation.2 | async-start | bytes 2097152 | tf_op jit(solution)/shard_map/all_to_all | solution.py:154
  41.3 31.0 %all-to-all-start = ((bf16[8,8,8704]{2,0,1:T(8,128)(2,1)}), bf16[8,8,8704]{2,0,1:T(8,128)(2,1)S(1)}, u32[]{:S(2)}, u32[]{:S(2)}) async-start(bf16[8,8,8704]{2,0,1:T(8,128)(2,1)} %pad_maximum_fusion), calls=%async_computation | async-start | bytes 2228224 | tf_op jit(solution)/shard_map/all_to_all | solution.py:154
  44.9 29.0 %collective-permute-start.9 = (bf16[64,8192]{1,0:T(8,128)(2,1)}, bf16[64,8192]{1,0:T(8,128)(2,1)}, u32[]{:S(2)}, u32[]{:S(2)}) collective-permute-start(bf16[64,8192]{1,0:T(8,128)(2,1)} %bitcast.22.refs_0_.refs_4_), channel_id=1, source_target_pairs={{0,16},{8,24},{16,0},{24,8},{1,17},{9,25},{17,1},{25,9},{2,18},{10... | collective-permute-start | bytes 3145736 | tf_op jit(solution)/shard_map/ppermute | solution.py:100
  47.4 52.2 %collective-permute-start.10 = (bf16[64,8192]{1,0:T(8,128)(2,1)}, bf16[64,8192]{1,0:T(8,128)(2,1)}, u32[]{:S(2)}, u32[]{:S(2)}) collective-permute-start(bf16[64,8192]{1,0:T(8,128)(2,1)} %bitcast.22.refs_0_.refs_4_), channel_id=1, source_target_pairs={{0,8},{8,0},{16,24},{24,16},{1,9},{9,1},{17,25},{25,17},{2,10},{10... | collective-permute-start | bytes 3145736 | tf_op jit(solution)/shard_map/ppermute | solution.py:100
  72.3 18.4 %collective-permute-start.6 = (bf16[64,6144]{1,0:T(8,128)(2,1)S(1)}, bf16[64,6144]{1,0:T(8,128)(2,1)S(1)}, u32[]{:S(2)}, u32[]{:S(2)}) collective-permute-start(bf16[64,6144]{1,0:T(8,128)(2,1)S(1)} %slice.133.refs_0_.refs_4_), channel_id=1, source_target_pairs={{0,16},{8,24},{16,0},{24,8},{1,17},{9,25},{17,1},{25,9},{2,18},{10... | collective-permute-start | bytes 2359304 | tf_op jit(solution)/shard_map/ppermute | solution.py:100
  73.9 26.1 %collective-permute-start.11 = (bf16[64,8192]{1,0:T(8,128)(2,1)}, bf16[64,8192]{1,0:T(8,128)(2,1)}, u32[]{:S(2)}, u32[]{:S(2)}) collective-permute-start(bf16[64,8192]{1,0:T(8,128)(2,1)} %collective-permute-done.9.refs_1_.refs_5_), channel_id=1, source_target_pairs={{0,8},{8,0},{16,24},{24,16},{1,9},{9,1},{17,25},{25,17},{2,10},{10... | collective-permute-start | bytes 3145736 | tf_op jit(solution)/shard_map/ppermute | solution.py:100
  74.6 16.2 %all-to-all-start.1 = ((bf16[8,8,2048]{2,0,1:T(8,128)(2,1)}), bf16[8,8,2048]{2,0,1:T(8,128)(2,1)S(1)}, u32[]{:S(2)}, u32[]{:S(2)}) async-start(bf16[8,8,2048]{2,0,1:T(8,128)(2,1)} %pad_maximum_fusion.3), calls=%async_computation.1 | async-start | bytes 524288 | tf_op jit(solution)/shard_map/all_to_all | solution.py:154
  78.3 2.9 %copy-start.2 = (bf16[64,640]{1,0:T(8,128)(2,1)}, bf16[64,640]{1,0:T(8,128)(2,1)S(1)}, u32[]{:S(2)}) copy-start(bf16[64,640]{1,0:T(8,128)(2,1)S(1)} %get-tuple-element.15) | copy-start | bytes 245764
  78.3 2.9 %copy-start.3 = (bf16[64,640]{1,0:T(8,128)(2,1)}, bf16[64,640]{1,0:T(8,128)(2,1)S(1)}, u32[]{:S(2)}) copy-start(bf16[64,640]{1,0:T(8,128)(2,1)S(1)} %get-tuple-element.16) | copy-start | bytes 245764
  78.3 2.9 %copy-start.4 = (bf16[64,640]{1,0:T(8,128)(2,1)}, bf16[64,640]{1,0:T(8,128)(2,1)S(1)}, u32[]{:S(2)}) copy-start(bf16[64,640]{1,0:T(8,128)(2,1)S(1)} %get-tuple-element.17) | copy-start | bytes 245764
  78.4 12.4 %copy-start = (bf16[256,640]{1,0:T(8,128)(2,1)}, bf16[256,640]{1,0:T(8,128)(2,1)S(1)}, u32[]{:S(2)}) copy-start(bf16[256,640]{1,0:T(8,128)(2,1)S(1)} %pad_maximum_fusion.2) | copy-start | bytes 983044
  79.2 11.6 %collective-permute-start.2 = (bf16[256,512]{1,0:T(8,128)(2,1)}, bf16[256,512]{1,0:T(8,128)(2,1)}, u32[]{:S(2)}, u32[]{:S(2)}) collective-permute-start(bf16[256,512]{1,0:T(8,128)(2,1)} %slice.130), channel_id=1, source_target_pairs={{0,1},{1,0},{2,3},{3,2},{4,5},{5,4},{6,7},{7,6},{8,9},{9,8},{10,11... | collective-permute-start | bytes 786440 | tf_op jit(solution)/shard_map/ppermute | solution.py:100
  81.2 32.6 %collective-permute-start.7 = (bf16[64,6144]{1,0:T(8,128)(2,1)S(1)}, bf16[64,6144]{1,0:T(8,128)(2,1)S(1)}, u32[]{:S(2)}, u32[]{:S(2)}) collective-permute-start(bf16[64,6144]{1,0:T(8,128)(2,1)S(1)} %slice.133.refs_0_.refs_4_), channel_id=1, source_target_pairs={{0,8},{8,0},{16,24},{24,16},{1,9},{9,1},{17,25},{25,17},{2,10},{10... | collective-permute-start | bytes 2359304 | tf_op jit(solution)/shard_map/ppermute | solution.py:100
  90.8 23.0 %collective-permute-start.8 = (bf16[64,6144]{1,0:T(8,128)(2,1)S(1)}, bf16[64,6144]{1,0:T(8,128)(2,1)S(1)}, u32[]{:S(2)}, u32[]{:S(2)}) collective-permute-start(bf16[64,6144]{1,0:T(8,128)(2,1)S(1)} %collective-permute-done.6.refs_1_.refs_5_), channel_id=1, source_target_pairs={{0,8},{8,0},{16,24},{24,16},{1,9},{9,1},{17,25},{25,17},{2,10},{10... | collective-permute-start | bytes 2359304 | tf_op jit(solution)/shard_map/ppermute | solution.py:100
  90.8 8.7 %collective-permute-start.3 = (bf16[64,2048]{1,0:T(8,128)(2,1)S(1)}, bf16[64,2048]{1,0:T(8,128)(2,1)S(1)}, u32[]{:S(2)}, u32[]{:S(2)}) collective-permute-start(bf16[64,2048]{1,0:T(8,128)(2,1)S(1)} %bitcast.38), channel_id=1, source_target_pairs={{0,16},{8,24},{16,0},{24,8},{1,17},{9,25},{17,1},{25,9},{2,18},{10... | collective-permute-start | bytes 786440 | tf_op jit(solution)/shard_map/ppermute | solution.py:100
  99.5 23.6 %collective-permute-start.4 = (bf16[64,2048]{1,0:T(8,128)(2,1)S(1)}, bf16[64,2048]{1,0:T(8,128)(2,1)S(1)}, u32[]{:S(2)}, u32[]{:S(2)}) collective-permute-start(bf16[64,2048]{1,0:T(8,128)(2,1)S(1)} %bitcast.39), channel_id=1, source_target_pairs={{0,8},{8,0},{16,24},{24,16},{1,9},{9,1},{17,25},{25,17},{2,10},{10... | collective-permute-start | bytes 786440 | tf_op jit(solution)/shard_map/ppermute | solution.py:100
  99.5 23.6 %collective-permute-start.5 = (bf16[64,2048]{1,0:T(8,128)(2,1)S(1)}, bf16[64,2048]{1,0:T(8,128)(2,1)S(1)}, u32[]{:S(2)}, u32[]{:S(2)}) collective-permute-start(bf16[64,2048]{1,0:T(8,128)(2,1)S(1)} %collective-permute-done.3.refs_1_.refs_5_), channel_id=1, source_target_pairs={{0,8},{8,0},{16,24},{24,16},{1,9},{9,1},{17,25},{25,17},{2,10},{10... | collective-permute-start | bytes 786440 | tf_op jit(solution)/shard_map/ppermute | solution.py:100

commit v2 on v1

v2 whole, which is shorter than its diff:
```python
import functools
import jax
import jax.numpy as jnp
from jax import lax
from jax.experimental import pallas as pl
from jax.experimental.pallas import tpu as pltpu
from jax.sharding import PartitionSpec as P

VMEM_BYTES = 40 * 1024 * 1024
PACK_BYTES = 58 * 1024 * 1024
LANES = 128
SHARES = (6, 7, 3)
GROUPS = ((0,), (1,), (2,))


def averaged(values, count):
    if count & (count - 1) == 0:
        return values * (1.0 / count)
    return values / count


def prepare_kernel(first_half, second_half, energy, row_out, shift_out):
    count = energy.shape[0]
    half = first_half.shape[1]
    for place, source in enumerate((first_half, second_half)):
        raw = source[...].astype(jnp.float32)
        centred = raw - averaged(jnp.sum(raw, axis=0, keepdims=True), count)
        row_out[place * half : (place + 1) * half, :] = centred.T.astype(jnp.bfloat16)
    parts = energy[...].astype(jnp.float32)
    value = (parts[:, 0:1] + parts[:, 1:2]) + parts[:, 2:3]
    shift = value - averaged(jnp.sum(value, axis=0, keepdims=True), count)
    shift_out[...] = jnp.broadcast_to(shift, shift_out.shape)


def prepare(first_half, second_half, energy):
    count, half = first_half.shape
    return pl.pallas_call(
        prepare_kernel,
        out_shape=(
            jax.ShapeDtypeStruct((2 * half, count), jnp.bfloat16),
            jax.ShapeDtypeStruct((count, LANES), jnp.float32),
        ),
        compiler_params=pltpu.CompilerParams(vmem_limit_bytes=VMEM_BYTES),
        cost_estimate=pl.CostEstimate(flops=4 * half * count, bytes_accessed=8 * half * count, transcendentals=0),
    )(first_half, second_half, energy)


def chunk_kernel(row_ref, shift_ref, *refs, pieces):
    derivs = refs[:pieces]
    grads = refs[pieces : 2 * pieces]
    correlation, hamiltonian, done = refs[-3:]
    done[...] = jnp.zeros_like(done)
    count = row_ref.shape[1]
    raw = jnp.concatenate([piece[...] for piece in derivs], axis=0).astype(jnp.float32)
    raw_grads = jnp.concatenate([piece[...] for piece in grads], axis=0).astype(jnp.float32)
    offsets = raw - averaged(jnp.sum(raw, axis=0, keepdims=True), count)
    grad_offsets = raw_grads - averaged(jnp.sum(raw_grads, axis=0, keepdims=True), count)
    centred = offsets.astype(jnp.bfloat16)
    term = (shift_ref[:, 0:1] * offsets + grad_offsets).astype(jnp.bfloat16)
    rows = row_ref[...]
    correlation[...] = averaged(jnp.dot(rows, centred, preferred_element_type=jnp.float32), count)
    hamiltonian[...] = averaged(jnp.dot(rows, term, preferred_element_type=jnp.float32), count)


def chunk_products(rows, shift, pieces, start, width, block, total_width, earlier):
    steps = width // block
    first = start // block
    n_rows = rows.shape[0]
    specs = [pl.BlockSpec(rows.shape, lambda j: (0, 0)), pl.BlockSpec(shift.shape, lambda j: (0, 0))]
    for offset in (0, steps):
        specs += [
            pl.BlockSpec((p.shape[0], block), lambda j, o=at // block + offset: (0, j + o)) for p, at in pieces
        ]
    arrays = [p for p, _ in pieces]
    operands = [rows, shift, *arrays, *arrays]
    aliases = {}
    if earlier is not None:
        aliases = {len(operands): 0, len(operands) + 1: 1}
        operands += list(earlier)
        specs += [pl.BlockSpec(memory_space=pl.ANY)] * 2
    return pl.pallas_call(
        functools.partial(chunk_kernel, pieces=len(pieces)),
        grid=(steps,),
        in_specs=specs,
        out_specs=[pl.BlockSpec((n_rows, block), lambda j: (0, j + first))] * 2
        + [pl.BlockSpec((8, LANES), lambda j: (0, 0))],
        out_shape=[jax.ShapeDtypeStruct((n_rows, total_width), jnp.float32)] * 2
        + [jax.ShapeDtypeStruct((8, LANES), jnp.float32)],
        input_output_aliases=aliases,
        compiler_params=pltpu.CompilerParams(vmem_limit_bytes=VMEM_BYTES),
        cost_estimate=pl.CostEstimate(
            flops=4 * n_rows * width * rows.shape[1], bytes_accessed=8 * n_rows * width, transcendentals=0
        ),
    )(*operands)


def pack_kernel(energy_ref, slab_ref, derivs_ref, grads_ref, *outs, peers, groups, tile, slab, rows):
    local = derivs_ref.shape[0]
    half = slab // (2 * rows)
    place = lax.broadcasted_iota(jnp.int32, (local, LANES), 0)
    lane = lax.broadcasted_iota(jnp.int32, (local, LANES), 1)
    value = jnp.zeros((local, LANES), jnp.float32)
    for sample in range(local):
        value = jnp.where(place == sample, energy_ref[sample], value)
    high = value.astype(jnp.bfloat16).astype(jnp.float32)
    rest = value - high
    middle = rest.astype(jnp.bfloat16).astype(jnp.float32)
    low = rest - middle
    tag = jnp.where(lane == 0, high, jnp.where(lane == 1, middle, jnp.where(lane == 2, low, 0.0)))
    tag = tag.astype(jnp.bfloat16)
    for number, (out, group) in enumerate(zip(outs, groups)):
        width = out.shape[1] // peers
        for peer in range(peers):
            at = peer * width
            for begin, end in group:
                for source in (derivs_ref, grads_ref):
                    out[:, at : at + end - begin] = source[:, peer * tile + begin : peer * tile + end]
                    at += end - begin
            if number == 0:
                for row in range(rows):
                    begin = (2 * row + peer % 2) * half
                    out[:, at : at + half] = slab_ref[:, begin : begin + half]
                    at += half
                out[:, at : at + LANES] = tag


def pack(energies, derivs, grads, peers, groups, slab, rows):
    local, width = derivs.shape
    tile = width // peers
    widths = [2 * sum(end - begin for begin, end in group) for group in groups]
    widths[0] += slab // 2 + LANES
    return pl.pallas_call(
        functools.partial(pack_kernel, peers=2, groups=groups, tile=tile, slab=slab, rows=rows),
        grid=(peers // 2,),
        in_specs=[
            pl.BlockSpec(memory_space=pltpu.SMEM),
            pl.BlockSpec((local, slab), lambda j: (0, 0)),
            pl.BlockSpec((local, 2 * tile), lambda j: (0, j)),
            pl.BlockSpec((local, 2 * tile), lambda j: (0, j)),
        ],
        out_specs=[pl.BlockSpec((local, 2 * w), lambda j: (0, j)) for w in widths],
        out_shape=[jax.ShapeDtypeStruct((local, peers * w), derivs.dtype) for w in widths],
        compiler_params=pltpu.CompilerParams(vmem_limit_bytes=PACK_BYTES),
    )(energies, derivs, derivs, grads)


def across(value, axis, distance):
    size = lax.axis_size(axis)
    return lax.ppermute(value, axis, [(i, i ^ distance) for i in range(size)])


def tied(value, *others):
    return lax.optimization_barrier((value, *others))[0]


def body(derivs, energy_derivs, energies):
    row_count = lax.axis_size("row")
    col_count = lax.axis_size("col")
    local = derivs.shape[0]
    total_width = derivs.shape[1] // col_count
    slab = derivs.shape[1] // 16
    row_width = slab // row_count
    half = row_width // 2
    row = lax.axis_index("row")
    odd = lax.axis_index("col") % 2

    unit = total_width // sum(SHARES)
    widths = [unit * s for s in SHARES]
    starts = [sum(widths[:i]) for i in range(len(widths))]
    block = min(512, unit)

    def to_owners(value):
        width = value.shape[1] // col_count
        tiles = value.reshape(value.shape[0], col_count, width)
        got = lax.all_to_all(tiles, "col", split_axis=1, concat_axis=0, tiled=True)
        return got.reshape(value.shape[0] * col_count, width)

    def take(value, index, width):
        return lax.dynamic_slice_in_dim(value, index * width, width, 1)

    def slab_pair(got):
        values, tags = got[:, : slab // 2], got[:, slab // 2 :]
        mine = jnp.concatenate((take(values, row // 2, 2 * half), tags), axis=1)
        sent = jnp.concatenate((take(values, 1 - row // 2, 2 * half), tags), axis=1)
        return jnp.concatenate((mine, across(sent, "row", 2)), axis=0)

    def slab_columns(pair):
        values, tags = pair[:, : 2 * half], pair[:, 2 * half :]
        mine = jnp.concatenate((take(values, row % 2, half), tags), axis=1)
        sent = jnp.concatenate((take(values, 1 - row % 2, half), tags), axis=1)
        quad = jnp.concatenate((mine, across(sent, "row", 1)), axis=0)
        return quad[:, :half], quad[:, half:]

    def slab_rows(held, tags):
        fetched = across(held, "col", 1)
        return prepare(jnp.where(odd == 0, held, fetched), jnp.where(odd == 0, fetched, held), tags)

    def products(i, pieces, outs):
        return chunk_products(rows, shift, pieces, starts[i], widths[i], block, total_width, outs)

    cuts = [(begin, begin + width) for begin, width in zip(starts, widths)]
    groups = [[cuts[i] for i in group] for group in GROUPS]
    sends = pack(energies, derivs, energy_derivs, col_count, groups, slab, row_count)
    last = len(widths) - 1
    wide = 2 * widths[last]
    last_far = across(sends[-1], "row", 2)
    joined = jnp.concatenate(
        (sends[-1].reshape(local, col_count, wide), last_far.reshape(local, col_count, wide)), axis=2
    )
    near, far = {}, {}

    def split(got, group):
        at = 0
        for i in group:
            near[i] = got[:, at : at + 2 * widths[i]]
            at += 2 * widths[i]
        return got[:, at:]

    first, joined = lax.optimization_barrier((to_owners(sends[0]), joined))
    pair = slab_pair(split(first, GROUPS[0]))
    held, tags = slab_columns(pair)
    rows, shift = slab_rows(held, tags)
    far[0] = tied(across(near[0], "row", 2), rows)
    for i in GROUPS[0][1:]:
        far[i] = across(near[i], "row", 2)
    for send, group in zip(sends[1:-1], GROUPS[1:-1]):
        split(to_owners(send), group)
        for i in group:
            far[i] = across(near[i], "row", 2)
    joined = joined.reshape(local, -1)
    joined = tied(joined, rows)
    ends = to_owners(joined)
    outs = done = None
    for i in range(len(widths)):
        if i == last:
            ends = tied(ends, begun)
            other = across(ends, "row", 1)
            pieces = [(ends, 0), (ends, wide), (other, 0), (other, wide)]
        else:
            if done is not None:
                far[i] = tied(far[i], done)
            pieces = [(near[i], 0), (far[i], 0), (across(near[i], "row", 1), 0), (across(far[i], "row", 1), 0)]
        *outs, done = products(i, pieces, outs)
        if i == 0:
            begun = done
    return tuple(outs)


def solution(mesh):
    placed = (P(("row", "col"), None), P(("row", "col"), None), P(("row", "col")))
    return jax.shard_map(
        body,
        mesh=mesh,
        in_specs=placed,
        out_specs=(P("row", "col"), P("row", "col")),
        check_vma=False,
    )
```

time: 129 us -> 111 us (0.86)
  waiting for transfers between devices: 63.5 us -> 47 us
  Pallas kernels: 27.6 us -> 32.1 us
  other arithmetic: 5.41 us -> 2.08 us
  starting transfers between devices: 23.6 us -> 21.9 us
    all_to_all x3, waiting for transfers between devices: 49.1 us -> 19.1 us  [to_owners(): got = lax.all_to_all(tiles, 'col', split_axis=1, concat_axis=0, tiled=True)]
    ppermute x12 -> x11, waiting for transfers between devices: 14.4 us -> 27.8 us  [across(): return lax.ppermute(value, axis, [(i, i ^ distance) for i in range(size)])]
    unnamed x24 -> x12, local copies, waits for them, and re-layouts: 0.21 us -> 5.35 us
    slice x10 -> x5, local copies, waits for them, and re-layouts: 5.87 us -> 1 us  [the longest x1 0.94 us: split(): near[i] = got[:, at:at + 2 * widths[i]]]
    pallas_call x0 -> x1, Pallas kernels: none -> 3.87 us  [pack(): pl.pallas_call(functools.partial(pack_kernel, peers=2, groups=groups, til...]
    ppermute x12 -> x11, starting transfers between devices: 10.3 us -> 6.64 us  [across(): return lax.ppermute(value, axis, [(i, i ^ distance) for i in range(size)])]
    all_to_all x3, starting transfers between devices: 13.3 us -> 15.3 us  [to_owners(): got = lax.all_to_all(tiles, 'col', split_axis=1, concat_axis=0, tiled=True)]
    concatenate x7 -> x5, other arithmetic: 2.91 us -> 2.03 us  [the longest x1 1.95 us: body(): jnp.concatenate((sends[-1].reshape(local, col_count, wide), last_far.resh...]
  transfers between devices with their start and end apart: 15 -> 14, of which waited for: 4 -> 8; matrix products, arithmetic and copies ran while one was open for 8% -> 3% of each run, Pallas kernels for 18% -> 21%
where the time goes in v2:
time: 111 us; the launch traced here: 110 us
  waiting for transfers between devices  47 us (42%)
  Pallas kernels  32.1 us (29%)
  starting transfers between devices  21.9 us (20%)
  local copies, waits for them, and re-layouts  6.41 us (6%)
  other arithmetic  2.08 us (2%)
    ppermute x11, waiting for transfers between devices, across(): return lax.ppermute(value, axis, [(i, i ^ distance) for i in range(size)])  27.8 us
    pallas_call x3, Pallas kernels, chunk_products(): pl.pallas_call(functools.partial(chunk_kernel, pieces=len(pieces)), grid=...  27.7 us
    all_to_all x3, waiting for transfers between devices, to_owners(): got = lax.all_to_all(tiles, 'col', split_axis=1, concat_axis=0, tiled=True)  19.1 us
    all_to_all x3, starting transfers between devices, to_owners(): got = lax.all_to_all(tiles, 'col', split_axis=1, concat_axis=0, tiled=True)  15.3 us
    ppermute x11, starting transfers between devices, across(): return lax.ppermute(value, axis, [(i, i ^ distance) for i in range(size)])  6.64 us
    unnamed x12, local copies, waits for them, and re-layouts  5.35 us
    pallas_call x1, Pallas kernels, pack(): pl.pallas_call(functools.partial(pack_kernel, peers=2, groups=groups, til...  3.87 us
  transfers between devices with their start and end apart: 14, of which 8 were waited for; matrix products, arithmetic and copies ran while one was open for 3% of the time, Pallas kernels for 21%

profile of v2, /device:TPU:0, one launch (start us, length us, event | category | flops | bytes accessed | tf_op | source)
XLA Modules:
  0.0 110.3 jit_solution(2120837327345040447)
XLA Ops:
  0.6 3.9 %shard_map.50 = (bf16[8,66560]{1,0:T(8,128)(2,1)}, bf16[8,57344]{1,0:T(8,128)(2,1)}, bf16[8,24576]{1,0:T(8,128)(2,1)}) custom-call(f32[8]{0:T(128)} %energy_ref.1, bf16[8,65536]{1,0:T(8,128)(2,1)} %derivs_ref.1, bf16[8,65536]{1,0:T(8,128)(2,1)} %derivs_ref.1, bf16[8,65536]{1,0:T(8,128)(2,1)} %grads_ref.1), custom_call_target="tpu_custom_call" | custom-call | tf_op jit(solution)/shard_map/pallas_call | solution.py:132
  4.5 7.3 %all-to-all-start = ((bf16[8,8,8320]{2,0,1:T(8,128)(2,1)}), bf16[8,8,8320]{2,0,1:T(8,128)(2,1)S(1)}, u32[]{:S(2)}, u32[]{:S(2)}) async-start(bf16[8,8,8320]{2,0,1:T(8,128)(2,1)} %bitcast.33), calls=%async_computation | async-start | bytes 2129920 | tf_op jit(solution)/shard_map/all_to_all | solution.py:175
  11.8 1.5 %collective-permute-start = (bf16[8,24576]{1,0:T(8,128)(2,1)}, bf16[8,24576]{1,0:T(8,128)(2,1)S(1)}, u32[]{:S(2)}, u32[]{:S(2)}) collective-permute-start(bf16[8,24576]{1,0:T(8,128)(2,1)} %get-tuple-element.21), channel_id=1, source_target_pairs={{0,16},{8,24},{16,0},{24,8},{1,17},{9,25},{17,1},{25,9},{2,18},{10... | collective-permute-start | bytes 1179656 | tf_op jit(solution)/shard_map/ppermute | solution.py:149
  13.3 9.3 %collective-permute-done = bf16[8,24576]{1,0:T(8,128)(2,1)S(1)} collective-permute-done((bf16[8,24576]{1,0:T(8,128)(2,1)}, bf16[8,24576]{1,0:T(8,128)(2,1)S(1)}, u32[]{:S(2)}, u32[]{:S(2)}) %collective-permute-start) | collective-permute-done | bytes 393248 | tf_op jit(solution)/shard_map/ppermute | solution.py:149
  22.6 1.9 %pad_maximum_fusion = bf16[8,8,6144]{2,0,1:T(8,128)(2,1)} fusion(bf16[8,8,3072]{2,0,1:T(8,128)(2,1)S(1)} %bitcast.36, bf16[8,8,3072]{2,0,1:T(8,128)(2,1)} %bitcast.35), kind=kLoop, calls=%fused_computation | loop fusion | flops 1572864 | bytes 1572864 | tf_op jit(solution)/shard_map/concatenate | solution.py:207
  24.5 13.4 %all-to-all-done = bf16[8,8,8320]{2,0,1:T(8,128)(2,1)S(1)} async-done(((bf16[8,8,8320]{2,0,1:T(8,128)(2,1)}), bf16[8,8,8320]{2,0,1:T(8,128)(2,1)S(1)}, u32[]{:S(2)}, u32[]{:S(2)}) %all-to-all-start) | async-done | bytes 1064992 | tf_op jit(solution)/shard_map/all_to_all | solution.py:175
  38.0 1.6 %collective-permute-start.1 = (bf16[64,1152]{1,0:T(8,128)(2,1)S(1)}, bf16[64,1152]{1,0:T(8,128)(2,1)S(1)}, u32[]{:S(2)}, u32[]{:S(2)}) collective-permute-start(bf16[64,1152]{1,0:T(8,128)(2,1)S(1)} %pad_maximum_fusion.4), channel_id=1, source_target_pairs={{0,16},{8,24},{16,0},{24,8},{1,17},{9,25},{17,1},{25,9},{2,18},{10... | collective-permute-start | bytes 442376 | tf_op jit(solution)/shard_map/ppermute | solution.py:149
  39.5 3.6 %all-to-all-start.2 = ((bf16[8,8,7168]{2,0,1:T(8,128)(2,1)}), bf16[8,8,7168]{2,0,1:T(8,128)(2,1)S(1)}, u32[]{:S(2)}, u32[]{:S(2)}) async-start(bf16[8,8,7168]{2,0,1:T(8,128)(2,1)} %bitcast.34), calls=%async_computation.2 | async-start | bytes 1835008 | tf_op jit(solution)/shard_map/all_to_all | solution.py:175
  43.1 0.1 collective-permute-done.1
  43.3 0.1 collective-permute-start.2
  43.4 0.9 slice.30.refs_0_.refs_4_
  44.3 1.5 %collective-permute-start.4 = (bf16[64,6144]{1,0:T(8,128)(2,1)}, bf16[64,6144]{1,0:T(8,128)(2,1)}, u32[]{:S(2)}, u32[]{:S(2)}) collective-permute-start(bf16[64,6144]{1,0:T(8,128)(2,1)} %slice.30.refs_0_.refs_4_), channel_id=1, source_target_pairs={{0,16},{8,24},{16,0},{24,8},{1,17},{9,25},{17,1},{25,9},{2,18},{10... | collective-permute-start | bytes 2359304 | tf_op jit(solution)/shard_map/ppermute | solution.py:149
  45.8 0.0 collective-permute-done.2
  45.9 1.5 %collective-permute-start.3 = (bf16[256,512]{1,0:T(8,128)(2,1)S(1)}, bf16[256,512]{1,0:T(8,128)(2,1)S(1)}, u32[]{:S(2)}, u32[]{:S(2)}) collective-permute-start(bf16[256,512]{1,0:T(8,128)(2,1)S(1)} %slice.32), channel_id=1, source_target_pairs={{0,1},{1,0},{2,3},{3,2},{4,5},{5,4},{6,7},{7,6},{8,9},{9,8},{10,11... | collective-permute-start | bytes 786440 | tf_op jit(solution)/shard_map/ppermute | solution.py:149
  47.4 12.9 %collective-permute-done.3 = bf16[256,512]{1,0:T(8,128)(2,1)S(1)} collective-permute-done((bf16[256,512]{1,0:T(8,128)(2,1)S(1)}, bf16[256,512]{1,0:T(8,128)(2,1)S(1)}, u32[]{:S(2)}, u32[]{:S(2)}) %collective-permute-start.3) | collective-permute-done | bytes 262176 | tf_op jit(solution)/shard_map/ppermute | solution.py:149
  60.3 0.5 shard_map.51
  60.8 0.8 copy-done
  61.6 0.6 copy-done.3
  62.3 2.3 %collective-permute-done.4.refs_1_.refs_5_ = bf16[64,6144]{1,0:T(8,128)(2,1)} collective-permute-done((bf16[64,6144]{1,0:T(8,128)(2,1)}, bf16[64,6144]{1,0:T(8,128)(2,1)}, u32[]{:S(2)}, u32[]{:S(2)}) %collective-permute-start.4) | collective-permute-done | bytes 786464 | tf_op jit(solution)/shard_map/ppermute | solution.py:149
  64.6 1.5 %all-to-all-done.2 = bf16[8,8,7168]{2,0,1:T(8,128)(2,1)S(1)} async-done(((bf16[8,8,7168]{2,0,1:T(8,128)(2,1)}), bf16[8,8,7168]{2,0,1:T(8,128)(2,1)S(1)}, u32[]{:S(2)}, u32[]{:S(2)}) %all-to-all-start.2) | async-done | bytes 917536 | tf_op jit(solution)/shard_map/all_to_all | solution.py:175
  66.1 0.5 collective-permute-start.8
  66.7 4.4 %all-to-all-start.1 = ((bf16[8,8,6144]{2,0,1:T(8,128)(2,1)}), bf16[8,8,6144]{2,0,1:T(8,128)(2,1)S(1)}, u32[]{:S(2)}, u32[]{:S(2)}) async-start(bf16[8,8,6144]{2,0,1:T(8,128)(2,1)} %bitcast.7), calls=%async_computation.1 | async-start | bytes 1572864 | tf_op jit(solution)/shard_map/all_to_all | solution.py:175
  71.1 0.0 collective-permute-start.9
  71.1 1.0 copy-done.1
  72.2 0.9 copy-done.4
  73.1 11.1 %shard_map.52 = (f32[1024,8192]{1,0:T(8,128)}, f32[1024,8192]{1,0:T(8,128)}, f32[8,128]{1,0:T(8,128)}) custom-call(bf16[1024,256]{1,0:T(8,128)(2,1)S(1)} %copy-done.1, f32[256,128]{1,0:T(8,128)S(1)} %copy-done.4, bf16[64,6144]{1,0:T(8,128)(2,1)} %slice.30.refs_0_.refs_4_, bf16[64,6144]{1,0:T(8,128)(2,1)} %collective-permute-done.4.refs_1_.refs_5_, ...), custom_call_target="tpu_custom_call" | custom-call | flops 3221225472 | bytes 25165824 | tf_op jit(solution)/shard_map/pallas_call | solution.py:81
  84.1 3.2 %collective-permute-done.8.refs_1_.refs_5_ = bf16[64,7168]{1,0:T(8,128)(2,1)S(1)} collective-permute-done((bf16[64,7168]{1,0:T(8,128)(2,1)S(1)}, bf16[64,7168]{1,0:T(8,128)(2,1)S(1)}, u32[]{:S(2)}, u32[]{:S(2)}) %collective-permute-start.8) | collective-permute-done | bytes 917536 | tf_op jit(solution)/shard_map/ppermute | solution.py:149
  87.4 4.3 %all-to-all-done.1 = bf16[8,8,6144]{2,0,1:T(8,128)(2,1)S(1)} async-done(((bf16[8,8,6144]{2,0,1:T(8,128)(2,1)}), bf16[8,8,6144]{2,0,1:T(8,128)(2,1)S(1)}, u32[]{:S(2)}, u32[]{:S(2)}) %all-to-all-start.1) | async-done | bytes 786464 | tf_op jit(solution)/shard_map/all_to_all | solution.py:175
  91.7 1.0 copy-done.2
  92.7 0.9 copy-done.5
  93.6 11.3 %shard_map.53 = (f32[1024,8192]{1,0:T(8,128)}, f32[1024,8192]{1,0:T(8,128)}, f32[8,128]{1,0:T(8,128)}) custom-call(bf16[1024,256]{1,0:T(8,128)(2,1)S(1)} %copy-done.2, f32[256,128]{1,0:T(8,128)S(1)} %copy-done.5, bf16[64,7168]{1,0:T(8,128)(2,1)S(1)} %bitcast.28, ...), custom_call_target="tpu_custom_call", output_to_operand_aliasing={{0}: (10, {}), {1}: (11, {})} | custom-call | flops 3758096384 | bytes 29360128 | tf_op jit(solution)/shard_map/pallas_call | solution.py:81
  104.9 5.4 %shard_map.54 = (f32[1024,8192]{1,0:T(8,128)}, f32[1024,8192]{1,0:T(8,128)}, f32[8,128]{1,0:T(8,128)}) custom-call(bf16[1024,256]{1,0:T(8,128)(2,1)S(1)} %copy-done.2, f32[256,128]{1,0:T(8,128)S(1)} %copy-done.5, bf16[64,6144]{1,0:T(8,128)(2,1)S(1)} %bitcast.22, bf16[64,6144]{1,0:T(8,128)(2,1)S(1)} %bitcast.23, ...), custom_call_target="tpu_custom_call", output_to_operand_aliasing={{0}: (10, {}), {1}: (11, {})} | custom-call | flops 1610612736 | bytes 12582912 | tf_op jit(solution)/shard_map/pallas_call | solution.py:81
  (28 shorter events, 0.3 us)
Async XLA Ops:
  4.5 33.4 %all-to-all-start = ((bf16[8,8,8320]{2,0,1:T(8,128)(2,1)}), bf16[8,8,8320]{2,0,1:T(8,128)(2,1)S(1)}, u32[]{:S(2)}, u32[]{:S(2)}) async-start(bf16[8,8,8320]{2,0,1:T(8,128)(2,1)} %bitcast.33), calls=%async_computation | async-start | bytes 2129920 | tf_op jit(solution)/shard_map/all_to_all | solution.py:175
  11.8 10.8 %collective-permute-start = (bf16[8,24576]{1,0:T(8,128)(2,1)}, bf16[8,24576]{1,0:T(8,128)(2,1)S(1)}, u32[]{:S(2)}, u32[]{:S(2)}) collective-permute-start(bf16[8,24576]{1,0:T(8,128)(2,1)} %get-tuple-element.21), channel_id=1, source_target_pairs={{0,16},{8,24},{16,0},{24,8},{1,17},{9,25},{17,1},{25,9},{2,18},{10... | collective-permute-start | bytes 1179656 | tf_op jit(solution)/shard_map/ppermute | solution.py:149
  38.0 5.2 %collective-permute-start.1 = (bf16[64,1152]{1,0:T(8,128)(2,1)S(1)}, bf16[64,1152]{1,0:T(8,128)(2,1)S(1)}, u32[]{:S(2)}, u32[]{:S(2)}) collective-permute-start(bf16[64,1152]{1,0:T(8,128)(2,1)S(1)} %pad_maximum_fusion.4), channel_id=1, source_target_pairs={{0,16},{8,24},{16,0},{24,8},{1,17},{9,25},{17,1},{25,9},{2,18},{10... | collective-permute-start | bytes 442376 | tf_op jit(solution)/shard_map/ppermute | solution.py:149
  39.5 26.6 %all-to-all-start.2 = ((bf16[8,8,7168]{2,0,1:T(8,128)(2,1)}), bf16[8,8,7168]{2,0,1:T(8,128)(2,1)S(1)}, u32[]{:S(2)}, u32[]{:S(2)}) async-start(bf16[8,8,7168]{2,0,1:T(8,128)(2,1)} %bitcast.34), calls=%async_computation.2 | async-start | bytes 1835008 | tf_op jit(solution)/shard_map/all_to_all | solution.py:175
  43.3 2.5 %collective-permute-start.2 = (bf16[128,640]{1,0:T(8,128)(2,1)S(1)}, bf16[128,640]{1,0:T(8,128)(2,1)S(1)}, u32[]{:S(2)}, u32[]{:S(2)}) collective-permute-start(bf16[128,640]{1,0:T(8,128)(2,1)S(1)} %pad_maximum_fusion.3), channel_id=1, source_target_pairs={{0,8},{8,0},{16,24},{24,16},{1,9},{9,1},{17,25},{25,17},{2,10},{10... | collective-permute-start | bytes 491528 | tf_op jit(solution)/shard_map/ppermute | solution.py:149
  44.3 20.3 %collective-permute-start.4 = (bf16[64,6144]{1,0:T(8,128)(2,1)}, bf16[64,6144]{1,0:T(8,128)(2,1)}, u32[]{:S(2)}, u32[]{:S(2)}) collective-permute-start(bf16[64,6144]{1,0:T(8,128)(2,1)} %slice.30.refs_0_.refs_4_), channel_id=1, source_target_pairs={{0,16},{8,24},{16,0},{24,8},{1,17},{9,25},{17,1},{25,9},{2,18},{10... | collective-permute-start | bytes 2359304 | tf_op jit(solution)/shard_map/ppermute | solution.py:149
  45.9 14.4 %collective-permute-start.3 = (bf16[256,512]{1,0:T(8,128)(2,1)S(1)}, bf16[256,512]{1,0:T(8,128)(2,1)S(1)}, u32[]{:S(2)}, u32[]{:S(2)}) collective-permute-start(bf16[256,512]{1,0:T(8,128)(2,1)S(1)} %slice.32), channel_id=1, source_target_pairs={{0,1},{1,0},{2,3},{3,2},{4,5},{5,4},{6,7},{7,6},{8,9},{9,8},{10,11... | collective-permute-start | bytes 786440 | tf_op jit(solution)/shard_map/ppermute | solution.py:149
  47.4 23.7 %collective-permute-start.5 = (bf16[64,6144]{1,0:T(8,128)(2,1)}, bf16[64,6144]{1,0:T(8,128)(2,1)}, u32[]{:S(2)}, u32[]{:S(2)}) collective-permute-start(bf16[64,6144]{1,0:T(8,128)(2,1)} %slice.30.refs_0_.refs_4_), channel_id=1, source_target_pairs={{0,8},{8,0},{16,24},{24,16},{1,9},{9,1},{17,25},{25,17},{2,10},{10... | collective-permute-start | bytes 2359304 | tf_op jit(solution)/shard_map/ppermute | solution.py:149
  60.8 0.8 copy-start
  61.6 0.6 copy-start.3
  64.6 6.5 %collective-permute-start.6 = (bf16[64,6144]{1,0:T(8,128)(2,1)}, bf16[64,6144]{1,0:T(8,128)(2,1)}, u32[]{:S(2)}, u32[]{:S(2)}) collective-permute-start(bf16[64,6144]{1,0:T(8,128)(2,1)} %collective-permute-done.4.refs_1_.refs_5_), channel_id=1, source_target_pairs={{0,8},{8,0},{16,24},{24,16},{1,9},{9,1},{17,25},{25,17},{2,10},{10... | collective-permute-start | bytes 2359304 | tf_op jit(solution)/shard_map/ppermute | solution.py:149
  66.1 21.3 %collective-permute-start.8 = (bf16[64,7168]{1,0:T(8,128)(2,1)S(1)}, bf16[64,7168]{1,0:T(8,128)(2,1)S(1)}, u32[]{:S(2)}, u32[]{:S(2)}) collective-permute-start(bf16[64,7168]{1,0:T(8,128)(2,1)S(1)} %bitcast.26), channel_id=1, source_target_pairs={{0,16},{8,24},{16,0},{24,8},{1,17},{9,25},{17,1},{25,9},{2,18},{10... | collective-permute-start | bytes 2752520 | tf_op jit(solution)/shard_map/ppermute | solution.py:149
  66.7 25.0 %all-to-all-start.1 = ((bf16[8,8,6144]{2,0,1:T(8,128)(2,1)}), bf16[8,8,6144]{2,0,1:T(8,128)(2,1)S(1)}, u32[]{:S(2)}, u32[]{:S(2)}) async-start(bf16[8,8,6144]{2,0,1:T(8,128)(2,1)} %bitcast.7), calls=%async_computation.1 | async-start | bytes 1572864 | tf_op jit(solution)/shard_map/all_to_all | solution.py:175
  71.1 20.5 %collective-permute-start.9 = (bf16[64,7168]{1,0:T(8,128)(2,1)S(1)}, bf16[64,7168]{1,0:T(8,128)(2,1)S(1)}, u32[]{:S(2)}, u32[]{:S(2)}) collective-permute-start(bf16[64,7168]{1,0:T(8,128)(2,1)S(1)} %bitcast.27), channel_id=1, source_target_pairs={{0,8},{8,0},{16,24},{24,16},{1,9},{9,1},{17,25},{25,17},{2,10},{10... | collective-permute-start | bytes 2752520 | tf_op jit(solution)/shard_map/ppermute | solution.py:149
  71.1 1.0 copy-start.1
  72.2 0.9 copy-start.4
  87.4 4.3 %collective-permute-start.10 = (bf16[64,7168]{1,0:T(8,128)(2,1)S(1)}, bf16[64,7168]{1,0:T(8,128)(2,1)}, u32[]{:S(2)}, u32[]{:S(2)}) collective-permute-start(bf16[64,7168]{1,0:T(8,128)(2,1)S(1)} %collective-permute-done.8.refs_1_.refs_5_), channel_id=1, source_target_pairs={{0,8},{8,0},{16,24},{24,16},{1,9},{9,1},{17,25},{25,17},{2,10},{10... | collective-permute-start | bytes 2752520 | tf_op jit(solution)/shard_map/ppermute | solution.py:149
  91.6 13.2 %collective-permute-start.7 = (bf16[64,6144]{1,0:T(8,128)(2,1)S(1)}, bf16[64,6144]{1,0:T(8,128)(2,1)S(1)}, u32[]{:S(2)}, u32[]{:S(2)}) collective-permute-start(bf16[64,6144]{1,0:T(8,128)(2,1)S(1)} %bitcast.21), channel_id=1, source_target_pairs={{0,8},{8,0},{16,24},{24,16},{1,9},{9,1},{17,25},{25,17},{2,10},{10... | collective-permute-start | bytes 2359304 | tf_op jit(solution)/shard_map/ppermute | solution.py:149
  91.6 1.0 copy-start.2
  92.7 0.9 copy-start.5

commit v3 on v2

--- a/solution.py
+++ b/solution.py
@@ -9,6 +9,7 @@
 VMEM_BYTES = 40 * 1024 * 1024
 PACK_BYTES = 58 * 1024 * 1024
 LANES = 128
+PACKED = 4
 SHARES = (6, 7, 3)
 GROUPS = ((0,), (1,), (2,))
 
@@ -130,15 +131,15 @@
     widths = [2 * sum(end - begin for begin, end in group) for group in groups]
     widths[0] += slab // 2 + LANES
     return pl.pallas_call(
-        functools.partial(pack_kernel, peers=2, groups=groups, tile=tile, slab=slab, rows=rows),
-        grid=(peers // 2,),
+        functools.partial(pack_kernel, peers=PACKED, groups=groups, tile=tile, slab=slab, rows=rows),
+        grid=(peers // PACKED,),
         in_specs=[
             pl.BlockSpec(memory_space=pltpu.SMEM),
             pl.BlockSpec((local, slab), lambda j: (0, 0)),
-            pl.BlockSpec((local, 2 * tile), lambda j: (0, j)),
-            pl.BlockSpec((local, 2 * tile), lambda j: (0, j)),
+            pl.BlockSpec((local, PACKED * tile), lambda j: (0, j)),
+            pl.BlockSpec((local, PACKED * tile), lambda j: (0, j)),
         ],
-        out_specs=[pl.BlockSpec((local, 2 * w), lambda j: (0, j)) for w in widths],
+        out_specs=[pl.BlockSpec((local, PACKED * w), lambda j: (0, j)) for w in widths],
         out_shape=[jax.ShapeDtypeStruct((local, peers * w), derivs.dtype) for w in widths],
         compiler_params=pltpu.CompilerParams(vmem_limit_bytes=PACK_BYTES),
     )(energies, derivs, derivs, grads)

time: 111 us -> 110 us (level)
  no operation moved by 1% of the time
where the time goes in v3:
time: 110 us; the launch traced here: 109 us
  waiting for transfers between devices  47 us (43%)
  Pallas kernels  31.1 us (28%)
  starting transfers between devices  21.9 us (20%)
  local copies, waits for them, and re-layouts  6.41 us (6%)
  other arithmetic  2.08 us (2%)
    ppermute x11, waiting for transfers between devices, across(): return lax.ppermute(value, axis, [(i, i ^ distance) for i in range(size)])  27.8 us
    pallas_call x3, Pallas kernels, chunk_products(): pl.pallas_call(functools.partial(chunk_kernel, pieces=len(pieces)), grid=...  27.7 us
    all_to_all x3, waiting for transfers between devices, to_owners(): got = lax.all_to_all(tiles, 'col', split_axis=1, concat_axis=0, tiled=True)  19.1 us
    all_to_all x3, starting transfers between devices, to_owners(): got = lax.all_to_all(tiles, 'col', split_axis=1, concat_axis=0, tiled=True)  15.3 us
    ppermute x11, starting transfers between devices, across(): return lax.ppermute(value, axis, [(i, i ^ distance) for i in range(size)])  6.64 us
    unnamed x12, local copies, waits for them, and re-layouts  5.35 us
    pallas_call x1, Pallas kernels, pack(): pl.pallas_call(functools.partial(pack_kernel, peers=PACKED, groups=groups...  2.87 us
  transfers between devices with their start and end apart: 14, of which 8 were waited for; matrix products, arithmetic and copies ran while one was open for 3% of the time, Pallas kernels for 21%

profile of v3, /device:TPU:0, one launch (start us, length us, event | category | flops | bytes accessed | tf_op | source)
XLA Modules:
  0.0 109.3 jit_solution(681805295922622484)
XLA Ops:
  0.6 2.9 %shard_map.50 = (bf16[8,66560]{1,0:T(8,128)(2,1)}, bf16[8,57344]{1,0:T(8,128)(2,1)}, bf16[8,24576]{1,0:T(8,128)(2,1)}) custom-call(f32[8]{0:T(128)} %energy_ref.1, bf16[8,65536]{1,0:T(8,128)(2,1)} %derivs_ref.1, bf16[8,65536]{1,0:T(8,128)(2,1)} %derivs_ref.1, bf16[8,65536]{1,0:T(8,128)(2,1)} %grads_ref.1), custom_call_target="tpu_custom_call" | custom-call | tf_op jit(solution)/shard_map/pallas_call | solution.py:133
  3.5 7.3 %all-to-all-start = ((bf16[8,8,8320]{2,0,1:T(8,128)(2,1)}), bf16[8,8,8320]{2,0,1:T(8,128)(2,1)S(1)}, u32[]{:S(2)}, u32[]{:S(2)}) async-start(bf16[8,8,8320]{2,0,1:T(8,128)(2,1)} %bitcast.33), calls=%async_computation | async-start | bytes 2129920 | tf_op jit(solution)/shard_map/all_to_all | solution.py:176
  10.8 1.5 %collective-permute-start = (bf16[8,24576]{1,0:T(8,128)(2,1)}, bf16[8,24576]{1,0:T(8,128)(2,1)S(1)}, u32[]{:S(2)}, u32[]{:S(2)}) collective-permute-start(bf16[8,24576]{1,0:T(8,128)(2,1)} %get-tuple-element.21), channel_id=1, source_target_pairs={{0,16},{8,24},{16,0},{24,8},{1,17},{9,25},{17,1},{25,9},{2,18},{10... | collective-permute-start | bytes 1179656 | tf_op jit(solution)/shard_map/ppermute | solution.py:150
  12.3 9.3 %collective-permute-done = bf16[8,24576]{1,0:T(8,128)(2,1)S(1)} collective-permute-done((bf16[8,24576]{1,0:T(8,128)(2,1)}, bf16[8,24576]{1,0:T(8,128)(2,1)S(1)}, u32[]{:S(2)}, u32[]{:S(2)}) %collective-permute-start) | collective-permute-done | bytes 393248 | tf_op jit(solution)/shard_map/ppermute | solution.py:150
  21.6 1.9 %pad_maximum_fusion = bf16[8,8,6144]{2,0,1:T(8,128)(2,1)} fusion(bf16[8,8,3072]{2,0,1:T(8,128)(2,1)S(1)} %bitcast.36, bf16[8,8,3072]{2,0,1:T(8,128)(2,1)} %bitcast.35), kind=kLoop, calls=%fused_computation | loop fusion | flops 1572864 | bytes 1572864 | tf_op jit(solution)/shard_map/concatenate | solution.py:208
  23.5 13.4 %all-to-all-done = bf16[8,8,8320]{2,0,1:T(8,128)(2,1)S(1)} async-done(((bf16[8,8,8320]{2,0,1:T(8,128)(2,1)}), bf16[8,8,8320]{2,0,1:T(8,128)(2,1)S(1)}, u32[]{:S(2)}, u32[]{:S(2)}) %all-to-all-start) | async-done | bytes 1064992 | tf_op jit(solution)/shard_map/all_to_all | solution.py:176
  37.0 1.6 %collective-permute-start.1 = (bf16[64,1152]{1,0:T(8,128)(2,1)S(1)}, bf16[64,1152]{1,0:T(8,128)(2,1)S(1)}, u32[]{:S(2)}, u32[]{:S(2)}) collective-permute-start(bf16[64,1152]{1,0:T(8,128)(2,1)S(1)} %pad_maximum_fusion.4), channel_id=1, source_target_pairs={{0,16},{8,24},{16,0},{24,8},{1,17},{9,25},{17,1},{25,9},{2,18},{10... | collective-permute-start | bytes 442376 | tf_op jit(solution)/shard_map/ppermute | solution.py:150
  38.5 3.6 %all-to-all-start.2 = ((bf16[8,8,7168]{2,0,1:T(8,128)(2,1)}), bf16[8,8,7168]{2,0,1:T(8,128)(2,1)S(1)}, u32[]{:S(2)}, u32[]{:S(2)}) async-start(bf16[8,8,7168]{2,0,1:T(8,128)(2,1)} %bitcast.34), calls=%async_computation.2 | async-start | bytes 1835008 | tf_op jit(solution)/shard_map/all_to_all | solution.py:176
  42.1 0.1 collective-permute-done.1
  42.3 0.1 collective-permute-start.2
  42.4 0.9 slice.30.refs_0_.refs_4_
  43.3 1.5 %collective-permute-start.4 = (bf16[64,6144]{1,0:T(8,128)(2,1)}, bf16[64,6144]{1,0:T(8,128)(2,1)}, u32[]{:S(2)}, u32[]{:S(2)}) collective-permute-start(bf16[64,6144]{1,0:T(8,128)(2,1)} %slice.30.refs_0_.refs_4_), channel_id=1, source_target_pairs={{0,16},{8,24},{16,0},{24,8},{1,17},{9,25},{17,1},{25,9},{2,18},{10... | collective-permute-start | bytes 2359304 | tf_op jit(solution)/shard_map/ppermute | solution.py:150
  44.8 0.0 collective-permute-done.2
  44.9 1.5 %collective-permute-start.3 = (bf16[256,512]{1,0:T(8,128)(2,1)S(1)}, bf16[256,512]{1,0:T(8,128)(2,1)S(1)}, u32[]{:S(2)}, u32[]{:S(2)}) collective-permute-start(bf16[256,512]{1,0:T(8,128)(2,1)S(1)} %slice.32), channel_id=1, source_target_pairs={{0,1},{1,0},{2,3},{3,2},{4,5},{5,4},{6,7},{7,6},{8,9},{9,8},{10,11... | collective-permute-start | bytes 786440 | tf_op jit(solution)/shard_map/ppermute | solution.py:150
  46.4 12.9 %collective-permute-done.3 = bf16[256,512]{1,0:T(8,128)(2,1)S(1)} collective-permute-done((bf16[256,512]{1,0:T(8,128)(2,1)S(1)}, bf16[256,512]{1,0:T(8,128)(2,1)S(1)}, u32[]{:S(2)}, u32[]{:S(2)}) %collective-permute-start.3) | collective-permute-done | bytes 262176 | tf_op jit(solution)/shard_map/ppermute | solution.py:150
  59.3 0.5 shard_map.51
  59.8 0.8 copy-done
  60.6 0.6 copy-done.3
  61.3 2.3 %collective-permute-done.4.refs_1_.refs_5_ = bf16[64,6144]{1,0:T(8,128)(2,1)} collective-permute-done((bf16[64,6144]{1,0:T(8,128)(2,1)}, bf16[64,6144]{1,0:T(8,128)(2,1)}, u32[]{:S(2)}, u32[]{:S(2)}) %collective-permute-start.4) | collective-permute-done | bytes 786464 | tf_op jit(solution)/shard_map/ppermute | solution.py:150
  63.6 0.0 collective-permute-start.6
  63.6 1.5 %all-to-all-done.2 = bf16[8,8,7168]{2,0,1:T(8,128)(2,1)S(1)} async-done(((bf16[8,8,7168]{2,0,1:T(8,128)(2,1)}), bf16[8,8,7168]{2,0,1:T(8,128)(2,1)S(1)}, u32[]{:S(2)}, u32[]{:S(2)}) %all-to-all-start.2) | async-done | bytes 917536 | tf_op jit(solution)/shard_map/all_to_all | solution.py:176
  65.1 0.5 collective-permute-start.8
  65.7 4.4 %all-to-all-start.1 = ((bf16[8,8,6144]{2,0,1:T(8,128)(2,1)}), bf16[8,8,6144]{2,0,1:T(8,128)(2,1)S(1)}, u32[]{:S(2)}, u32[]{:S(2)}) async-start(bf16[8,8,6144]{2,0,1:T(8,128)(2,1)} %bitcast.7), calls=%async_computation.1 | async-start | bytes 1572864 | tf_op jit(solution)/shard_map/all_to_all | solution.py:176
  70.1 1.0 copy-done.1
  71.2 0.9 copy-done.4
  72.1 11.1 %shard_map.52 = (f32[1024,8192]{1,0:T(8,128)}, f32[1024,8192]{1,0:T(8,128)}, f32[8,128]{1,0:T(8,128)}) custom-call(bf16[1024,256]{1,0:T(8,128)(2,1)S(1)} %copy-done.1, f32[256,128]{1,0:T(8,128)S(1)} %copy-done.4, bf16[64,6144]{1,0:T(8,128)(2,1)} %slice.30.refs_0_.refs_4_, bf16[64,6144]{1,0:T(8,128)(2,1)} %collective-permute-done.4.refs_1_.refs_5_, ...), custom_call_target="tpu_custom_call" | custom-call | flops 3221225472 | bytes 25165824 | tf_op jit(solution)/shard_map/pallas_call | solution.py:82
  83.1 3.2 %collective-permute-done.8.refs_1_.refs_5_ = bf16[64,7168]{1,0:T(8,128)(2,1)S(1)} collective-permute-done((bf16[64,7168]{1,0:T(8,128)(2,1)S(1)}, bf16[64,7168]{1,0:T(8,128)(2,1)S(1)}, u32[]{:S(2)}, u32[]{:S(2)}) %collective-permute-start.8) | collective-permute-done | bytes 917536 | tf_op jit(solution)/shard_map/ppermute | solution.py:150
  86.4 4.3 %all-to-all-done.1 = bf16[8,8,6144]{2,0,1:T(8,128)(2,1)S(1)} async-done(((bf16[8,8,6144]{2,0,1:T(8,128)(2,1)}), bf16[8,8,6144]{2,0,1:T(8,128)(2,1)S(1)}, u32[]{:S(2)}, u32[]{:S(2)}) %all-to-all-start.1) | async-done | bytes 786464 | tf_op jit(solution)/shard_map/all_to_all | solution.py:176
  90.7 1.0 copy-done.2
  91.7 0.9 copy-done.5
  92.6 11.3 %shard_map.53 = (f32[1024,8192]{1,0:T(8,128)}, f32[1024,8192]{1,0:T(8,128)}, f32[8,128]{1,0:T(8,128)}) custom-call(bf16[1024,256]{1,0:T(8,128)(2,1)S(1)} %copy-done.2, f32[256,128]{1,0:T(8,128)S(1)} %copy-done.5, bf16[64,7168]{1,0:T(8,128)(2,1)S(1)} %bitcast.28, ...), custom_call_target="tpu_custom_call", output_to_operand_aliasing={{0}: (10, {}), {1}: (11, {})} | custom-call | flops 3758096384 | bytes 29360128 | tf_op jit(solution)/shard_map/pallas_call | solution.py:82
  103.9 5.4 %shard_map.54 = (f32[1024,8192]{1,0:T(8,128)}, f32[1024,8192]{1,0:T(8,128)}, f32[8,128]{1,0:T(8,128)}) custom-call(bf16[1024,256]{1,0:T(8,128)(2,1)S(1)} %copy-done.2, f32[256,128]{1,0:T(8,128)S(1)} %copy-done.5, bf16[64,6144]{1,0:T(8,128)(2,1)S(1)} %bitcast.22, bf16[64,6144]{1,0:T(8,128)(2,1)S(1)} %bitcast.23, ...), custom_call_target="tpu_custom_call", output_to_operand_aliasing={{0}: (10, {}), {1}: (11, {})} | custom-call | flops 1610612736 | bytes 12582912 | tf_op jit(solution)/shard_map/pallas_call | solution.py:82
  (28 shorter events, 0.3 us)
Async XLA Ops:
  3.5 33.4 %all-to-all-start = ((bf16[8,8,8320]{2,0,1:T(8,128)(2,1)}), bf16[8,8,8320]{2,0,1:T(8,128)(2,1)S(1)}, u32[]{:S(2)}, u32[]{:S(2)}) async-start(bf16[8,8,8320]{2,0,1:T(8,128)(2,1)} %bitcast.33), calls=%async_computation | async-start | bytes 2129920 | tf_op jit(solution)/shard_map/all_to_all | solution.py:176
  10.8 10.8 %collective-permute-start = (bf16[8,24576]{1,0:T(8,128)(2,1)}, bf16[8,24576]{1,0:T(8,128)(2,1)S(1)}, u32[]{:S(2)}, u32[]{:S(2)}) collective-permute-start(bf16[8,24576]{1,0:T(8,128)(2,1)} %get-tuple-element.21), channel_id=1, source_target_pairs={{0,16},{8,24},{16,0},{24,8},{1,17},{9,25},{17,1},{25,9},{2,18},{10... | collective-permute-start | bytes 1179656 | tf_op jit(solution)/shard_map/ppermute | solution.py:150
  37.0 5.2 %collective-permute-start.1 = (bf16[64,1152]{1,0:T(8,128)(2,1)S(1)}, bf16[64,1152]{1,0:T(8,128)(2,1)S(1)}, u32[]{:S(2)}, u32[]{:S(2)}) collective-permute-start(bf16[64,1152]{1,0:T(8,128)(2,1)S(1)} %pad_maximum_fusion.4), channel_id=1, source_target_pairs={{0,16},{8,24},{16,0},{24,8},{1,17},{9,25},{17,1},{25,9},{2,18},{10... | collective-permute-start | bytes 442376 | tf_op jit(solution)/shard_map/ppermute | solution.py:150
  38.5 26.6 %all-to-all-start.2 = ((bf16[8,8,7168]{2,0,1:T(8,128)(2,1)}), bf16[8,8,7168]{2,0,1:T(8,128)(2,1)S(1)}, u32[]{:S(2)}, u32[]{:S(2)}) async-start(bf16[8,8,7168]{2,0,1:T(8,128)(2,1)} %bitcast.34), calls=%async_computation.2 | async-start | bytes 1835008 | tf_op jit(solution)/shard_map/all_to_all | solution.py:176
  42.3 2.5 %collective-permute-start.2 = (bf16[128,640]{1,0:T(8,128)(2,1)S(1)}, bf16[128,640]{1,0:T(8,128)(2,1)S(1)}, u32[]{:S(2)}, u32[]{:S(2)}) collective-permute-start(bf16[128,640]{1,0:T(8,128)(2,1)S(1)} %pad_maximum_fusion.3), channel_id=1, source_target_pairs={{0,8},{8,0},{16,24},{24,16},{1,9},{9,1},{17,25},{25,17},{2,10},{10... | collective-permute-start | bytes 491528 | tf_op jit(solution)/shard_map/ppermute | solution.py:150
  43.3 20.3 %collective-permute-start.4 = (bf16[64,6144]{1,0:T(8,128)(2,1)}, bf16[64,6144]{1,0:T(8,128)(2,1)}, u32[]{:S(2)}, u32[]{:S(2)}) collective-permute-start(bf16[64,6144]{1,0:T(8,128)(2,1)} %slice.30.refs_0_.refs_4_), channel_id=1, source_target_pairs={{0,16},{8,24},{16,0},{24,8},{1,17},{9,25},{17,1},{25,9},{2,18},{10... | collective-permute-start | bytes 2359304 | tf_op jit(solution)/shard_map/ppermute | solution.py:150
  44.9 14.4 %collective-permute-start.3 = (bf16[256,512]{1,0:T(8,128)(2,1)S(1)}, bf16[256,512]{1,0:T(8,128)(2,1)S(1)}, u32[]{:S(2)}, u32[]{:S(2)}) collective-permute-start(bf16[256,512]{1,0:T(8,128)(2,1)S(1)} %slice.32), channel_id=1, source_target_pairs={{0,1},{1,0},{2,3},{3,2},{4,5},{5,4},{6,7},{7,6},{8,9},{9,8},{10,11... | collective-permute-start | bytes 786440 | tf_op jit(solution)/shard_map/ppermute | solution.py:150
  46.4 23.7 %collective-permute-start.5 = (bf16[64,6144]{1,0:T(8,128)(2,1)}, bf16[64,6144]{1,0:T(8,128)(2,1)}, u32[]{:S(2)}, u32[]{:S(2)}) collective-permute-start(bf16[64,6144]{1,0:T(8,128)(2,1)} %slice.30.refs_0_.refs_4_), channel_id=1, source_target_pairs={{0,8},{8,0},{16,24},{24,16},{1,9},{9,1},{17,25},{25,17},{2,10},{10... | collective-permute-start | bytes 2359304 | tf_op jit(solution)/shard_map/ppermute | solution.py:150
  59.8 0.8 copy-start
  60.6 0.6 copy-start.3
  63.6 6.5 %collective-permute-start.6 = (bf16[64,6144]{1,0:T(8,128)(2,1)}, bf16[64,6144]{1,0:T(8,128)(2,1)}, u32[]{:S(2)}, u32[]{:S(2)}) collective-permute-start(bf16[64,6144]{1,0:T(8,128)(2,1)} %collective-permute-done.4.refs_1_.refs_5_), channel_id=1, source_target_pairs={{0,8},{8,0},{16,24},{24,16},{1,9},{9,1},{17,25},{25,17},{2,10},{10... | collective-permute-start | bytes 2359304 | tf_op jit(solution)/shard_map/ppermute | solution.py:150
  65.1 21.3 %collective-permute-start.8 = (bf16[64,7168]{1,0:T(8,128)(2,1)S(1)}, bf16[64,7168]{1,0:T(8,128)(2,1)S(1)}, u32[]{:S(2)}, u32[]{:S(2)}) collective-permute-start(bf16[64,7168]{1,0:T(8,128)(2,1)S(1)} %bitcast.26), channel_id=1, source_target_pairs={{0,16},{8,24},{16,0},{24,8},{1,17},{9,25},{17,1},{25,9},{2,18},{10... | collective-permute-start | bytes 2752520 | tf_op jit(solution)/shard_map/ppermute | solution.py:150
  65.7 25.0 %all-to-all-start.1 = ((bf16[8,8,6144]{2,0,1:T(8,128)(2,1)}), bf16[8,8,6144]{2,0,1:T(8,128)(2,1)S(1)}, u32[]{:S(2)}, u32[]{:S(2)}) async-start(bf16[8,8,6144]{2,0,1:T(8,128)(2,1)} %bitcast.7), calls=%async_computation.1 | async-start | bytes 1572864 | tf_op jit(solution)/shard_map/all_to_all | solution.py:176
  70.1 20.5 %collective-permute-start.9 = (bf16[64,7168]{1,0:T(8,128)(2,1)S(1)}, bf16[64,7168]{1,0:T(8,128)(2,1)S(1)}, u32[]{:S(2)}, u32[]{:S(2)}) collective-permute-start(bf16[64,7168]{1,0:T(8,128)(2,1)S(1)} %bitcast.27), channel_id=1, source_target_pairs={{0,8},{8,0},{16,24},{24,16},{1,9},{9,1},{17,25},{25,17},{2,10},{10... | collective-permute-start | bytes 2752520 | tf_op jit(solution)/shard_map/ppermute | solution.py:150
  70.1 1.0 copy-start.1
  71.2 0.9 copy-start.4
  86.4 4.3 %collective-permute-start.10 = (bf16[64,7168]{1,0:T(8,128)(2,1)S(1)}, bf16[64,7168]{1,0:T(8,128)(2,1)}, u32[]{:S(2)}, u32[]{:S(2)}) collective-permute-start(bf16[64,7168]{1,0:T(8,128)(2,1)S(1)} %collective-permute-done.8.refs_1_.refs_5_), channel_id=1, source_target_pairs={{0,8},{8,0},{16,24},{24,16},{1,9},{9,1},{17,25},{25,17},{2,10},{10... | collective-permute-start | bytes 2752520 | tf_op jit(solution)/shard_map/ppermute | solution.py:150
  90.6 13.2 %collective-permute-start.7 = (bf16[64,6144]{1,0:T(8,128)(2,1)S(1)}, bf16[64,6144]{1,0:T(8,128)(2,1)S(1)}, u32[]{:S(2)}, u32[]{:S(2)}) collective-permute-start(bf16[64,6144]{1,0:T(8,128)(2,1)S(1)} %bitcast.21), channel_id=1, source_target_pairs={{0,8},{8,0},{16,24},{24,16},{1,9},{9,1},{17,25},{25,17},{2,10},{10... | collective-permute-start | bytes 2359304 | tf_op jit(solution)/shard_map/ppermute | solution.py:150
  90.6 1.0 copy-start.2
  91.7 0.9 copy-start.5

commit v4 on v3

--- a/solution.py
+++ b/solution.py
@@ -10,7 +10,7 @@
 PACK_BYTES = 58 * 1024 * 1024
 LANES = 128
 PACKED = 4
-SHARES = (6, 7, 3)
+SHARES = (7, 7, 2)
 GROUPS = ((0,), (1,), (2,))
 
 

time: 110 us -> 112 us (1.018)
  local copies, waits for them, and re-layouts: 6.41 us -> 3.99 us
  waiting for transfers between devices: 47 us -> 48.9 us
  starting transfers between devices: 21.9 us -> 23.7 us
    unnamed x12 -> x6, local copies, waits for them, and re-layouts: 5.35 us -> 2.88 us
    ppermute x11, waiting for transfers between devices: 27.8 us -> 29.7 us  [across(): return lax.ppermute(value, axis, [(i, i ^ distance) for i in range(size)])]
    all_to_all x3, starting transfers between devices: 15.3 us -> 16.6 us  [to_owners(): got = lax.all_to_all(tiles, 'col', split_axis=1, concat_axis=0, tiled=True)]
  transfers between devices with their start and end apart: 14 -> 14, of which waited for: 8 -> 7; matrix products, arithmetic and copies ran while one was open for 3% -> 3% of each run, Pallas kernels for 21% -> 22%
where the time goes in v4:
time: 112 us; the launch traced here: 111 us
  waiting for transfers between devices  48.9 us (44%)
  Pallas kernels  31.4 us (28%)
  starting transfers between devices  23.7 us (21%)
  local copies, waits for them, and re-layouts  3.99 us (4%)
  other arithmetic  1.9 us (2%)
    ppermute x11, waiting for transfers between devices, across(): return lax.ppermute(value, axis, [(i, i ^ distance) for i in range(size)])  29.7 us
    pallas_call x3, Pallas kernels, chunk_products(): pl.pallas_call(functools.partial(chunk_kernel, pieces=len(pieces)), grid=...  28.1 us
    all_to_all x3, waiting for transfers between devices, to_owners(): got = lax.all_to_all(tiles, 'col', split_axis=1, concat_axis=0, tiled=True)  19.2 us
    all_to_all x3, starting transfers between devices, to_owners(): got = lax.all_to_all(tiles, 'col', split_axis=1, concat_axis=0, tiled=True)  16.6 us
    ppermute x11, starting transfers between devices, across(): return lax.ppermute(value, axis, [(i, i ^ distance) for i in range(size)])  7.02 us
    unnamed x6, local copies, waits for them, and re-layouts  2.88 us
    pallas_call x1, Pallas kernels, pack(): pl.pallas_call(functools.partial(pack_kernel, peers=PACKED, groups=groups...  2.86 us
  transfers between devices with their start and end apart: 14, of which 7 were waited for; matrix products, arithmetic and copies ran while one was open for 3% of the time, Pallas kernels for 22%

profile of v4, /device:TPU:0, one launch (start us, length us, event | category | flops | bytes accessed | tf_op | source)
XLA Modules:
  0.0 110.6 jit_solution(16677239519219015073)
XLA Ops:
  0.6 2.9 %shard_map.50 = (bf16[8,74752]{1,0:T(8,128)(2,1)}, bf16[8,57344]{1,0:T(8,128)(2,1)}, bf16[8,16384]{1,0:T(8,128)(2,1)}) custom-call(f32[8]{0:T(128)} %energy_ref.1, bf16[8,65536]{1,0:T(8,128)(2,1)} %derivs_ref.1, bf16[8,65536]{1,0:T(8,128)(2,1)} %derivs_ref.1, bf16[8,65536]{1,0:T(8,128)(2,1)} %grads_ref.1), custom_call_target="tpu_custom_call" | custom-call | tf_op jit(solution)/shard_map/pallas_call | solution.py:133
  3.5 7.3 %all-to-all-start = ((bf16[8,8,9344]{2,0,1:T(8,128)(2,1)}), bf16[8,8,9344]{2,0,1:T(8,128)(2,1)S(1)}, u32[]{:S(2)}, u32[]{:S(2)}) async-start(bf16[8,8,9344]{2,0,1:T(8,128)(2,1)} %bitcast.33), calls=%async_computation | async-start | bytes 2392064 | tf_op jit(solution)/shard_map/all_to_all | solution.py:176
  10.8 1.5 %collective-permute-start = (bf16[8,16384]{1,0:T(8,128)(2,1)}, bf16[8,16384]{1,0:T(8,128)(2,1)S(1)}, u32[]{:S(2)}, u32[]{:S(2)}) collective-permute-start(bf16[8,16384]{1,0:T(8,128)(2,1)} %get-tuple-element.21), channel_id=1, source_target_pairs={{0,16},{8,24},{16,0},{24,8},{1,17},{9,25},{17,1},{25,9},{2,18},{10... | collective-permute-start | bytes 786440 | tf_op jit(solution)/shard_map/ppermute | solution.py:150
  12.3 6.5 %collective-permute-done = bf16[8,16384]{1,0:T(8,128)(2,1)S(1)} collective-permute-done((bf16[8,16384]{1,0:T(8,128)(2,1)}, bf16[8,16384]{1,0:T(8,128)(2,1)S(1)}, u32[]{:S(2)}, u32[]{:S(2)}) %collective-permute-start) | collective-permute-done | bytes 262176 | tf_op jit(solution)/shard_map/ppermute | solution.py:150
  18.8 1.8 %pad_maximum_fusion = bf16[8,8,4096]{2,0,1:T(8,128)(2,1)} fusion(bf16[8,8,2048]{2,0,1:T(8,128)(2,1)S(1)} %bitcast.36, bf16[8,8,2048]{2,0,1:T(8,128)(2,1)} %bitcast.35), kind=kLoop, calls=%fused_computation | loop fusion | flops 1048576 | bytes 1048576 | tf_op jit(solution)/shard_map/concatenate | solution.py:208
  20.5 19.2 %all-to-all-done = bf16[8,8,9344]{2,0,1:T(8,128)(2,1)S(1)} async-done(((bf16[8,8,9344]{2,0,1:T(8,128)(2,1)}), bf16[8,8,9344]{2,0,1:T(8,128)(2,1)S(1)}, u32[]{:S(2)}, u32[]{:S(2)}) %all-to-all-start) | async-done | bytes 1196064 | tf_op jit(solution)/shard_map/all_to_all | solution.py:176
  39.8 1.6 %collective-permute-start.1 = (bf16[64,1152]{1,0:T(8,128)(2,1)S(1)}, bf16[64,1152]{1,0:T(8,128)(2,1)S(1)}, u32[]{:S(2)}, u32[]{:S(2)}) collective-permute-start(bf16[64,1152]{1,0:T(8,128)(2,1)S(1)} %pad_maximum_fusion.4), channel_id=1, source_target_pairs={{0,16},{8,24},{16,0},{24,8},{1,17},{9,25},{17,1},{25,9},{2,18},{10... | collective-permute-start | bytes 442376 | tf_op jit(solution)/shard_map/ppermute | solution.py:150
  41.3 3.6 %all-to-all-start.2 = ((bf16[8,8,7168]{2,0,1:T(8,128)(2,1)}), bf16[8,8,7168]{2,0,1:T(8,128)(2,1)S(1)}, u32[]{:S(2)}, u32[]{:S(2)}) async-start(bf16[8,8,7168]{2,0,1:T(8,128)(2,1)} %bitcast.34), calls=%async_computation.2 | async-start | bytes 1835008 | tf_op jit(solution)/shard_map/all_to_all | solution.py:176
  45.0 1.0 slice.30.refs_0_.refs_4_
  46.0 0.5 collective-permute-start.4
  46.6 0.1 collective-permute-start.2
  46.7 1.4 %collective-permute-done.2 = bf16[128,640]{1,0:T(8,128)(2,1)S(1)} collective-permute-done((bf16[128,640]{1,0:T(8,128)(2,1)S(1)}, bf16[128,640]{1,0:T(8,128)(2,1)S(1)}, u32[]{:S(2)}, u32[]{:S(2)}) %collective-permute-start.2) | collective-permute-done | bytes 163872 | tf_op jit(solution)/shard_map/ppermute | solution.py:150
  48.2 2.1 %collective-permute-start.3 = (bf16[256,512]{1,0:T(8,128)(2,1)S(1)}, bf16[256,512]{1,0:T(8,128)(2,1)S(1)}, u32[]{:S(2)}, u32[]{:S(2)}) collective-permute-start(bf16[256,512]{1,0:T(8,128)(2,1)S(1)} %slice.32), channel_id=1, source_target_pairs={{0,1},{1,0},{2,3},{3,2},{4,5},{5,4},{6,7},{7,6},{8,9},{9,8},{10,11... | collective-permute-start | bytes 786440 | tf_op jit(solution)/shard_map/ppermute | solution.py:150
  50.3 11.9 %collective-permute-done.3 = bf16[256,512]{1,0:T(8,128)(2,1)S(1)} collective-permute-done((bf16[256,512]{1,0:T(8,128)(2,1)S(1)}, bf16[256,512]{1,0:T(8,128)(2,1)S(1)}, u32[]{:S(2)}, u32[]{:S(2)}) %collective-permute-start.3) | collective-permute-done | bytes 262176 | tf_op jit(solution)/shard_map/ppermute | solution.py:150
  62.2 0.5 shard_map.51
  62.7 0.8 copy-done
  63.5 4.6 %collective-permute-done.4.refs_1_.refs_5_ = bf16[64,7168]{1,0:T(8,128)(2,1)} collective-permute-done((bf16[64,7168]{1,0:T(8,128)(2,1)}, bf16[64,7168]{1,0:T(8,128)(2,1)}, u32[]{:S(2)}, u32[]{:S(2)}) %collective-permute-start.4) | collective-permute-done | bytes 917536 | tf_op jit(solution)/shard_map/ppermute | solution.py:150
  68.0 0.0 collective-permute-start.6
  68.0 0.0 all-to-all-done.2
  68.0 0.5 collective-permute-start.8
  68.6 0.2 collective-permute-start.9
  68.8 5.7 %all-to-all-start.1 = ((bf16[8,8,4096]{2,0,1:T(8,128)(2,1)}), bf16[8,8,4096]{2,0,1:T(8,128)(2,1)S(1)}, u32[]{:S(2)}, u32[]{:S(2)}) async-start(bf16[8,8,4096]{2,0,1:T(8,128)(2,1)} %pad_maximum_fusion), calls=%async_computation.1 | async-start | bytes 1048576 | tf_op jit(solution)/shard_map/all_to_all | solution.py:176
  74.5 0.0 collective-permute-done.5.refs_2_.refs_6_
  74.5 1.0 copy-done.1
  75.6 12.7 %shard_map.52 = (f32[1024,8192]{1,0:T(8,128)}, f32[1024,8192]{1,0:T(8,128)}, f32[8,128]{1,0:T(8,128)}) custom-call(bf16[1024,256]{1,0:T(8,128)(2,1)S(1)} %copy-done.1, f32[256,128]{1,0:T(8,128)S(1)} %get-tuple-element.24.shift_ref, bf16[64,7168]{1,0:T(8,128)(2,1)} %slice.30.refs_0_.refs_4_, bf16[64,7168]{1,0:T(8,128)(2,1)} %collective-permute-done.4.refs_1_.refs_5_, ...), custom_call_target="tpu_custom_call" | custom-call | flops 3758096384 | bytes 29360128 | tf_op jit(solution)/shard_map/pallas_call | solution.py:82
  88.2 2.5 %collective-permute-done.8.refs_1_.refs_5_ = bf16[64,7168]{1,0:T(8,128)(2,1)S(1)} collective-permute-done((bf16[64,7168]{1,0:T(8,128)(2,1)S(1)}, bf16[64,7168]{1,0:T(8,128)(2,1)S(1)}, u32[]{:S(2)}, u32[]{:S(2)}) %collective-permute-start.8) | collective-permute-done | bytes 917536 | tf_op jit(solution)/shard_map/ppermute | solution.py:150
  90.8 0.0 collective-permute-start.10
  90.8 0.5 collective-permute-start.7
  91.3 2.8 %collective-permute-done.10.refs_3_.refs_7_ = bf16[64,7168]{1,0:T(8,128)(2,1)} collective-permute-done((bf16[64,7168]{1,0:T(8,128)(2,1)S(1)}, bf16[64,7168]{1,0:T(8,128)(2,1)}, u32[]{:S(2)}, u32[]{:S(2)}) %collective-permute-start.10) | collective-permute-done | bytes 917536 | tf_op jit(solution)/shard_map/ppermute | solution.py:150
  94.1 1.0 copy-done.2
  95.2 11.3 %shard_map.53 = (f32[1024,8192]{1,0:T(8,128)}, f32[1024,8192]{1,0:T(8,128)}, f32[8,128]{1,0:T(8,128)}) custom-call(bf16[1024,256]{1,0:T(8,128)(2,1)S(1)} %copy-done.2, f32[256,128]{1,0:T(8,128)S(1)} %get-tuple-element.24.shift_ref, bf16[64,7168]{1,0:T(8,128)(2,1)S(1)} %bitcast.28, ...), custom_call_target="tpu_custom_call", output_to_operand_aliasing={{0}: (10, {}), {1}: (11, {})} | custom-call | flops 3758096384 | bytes 29360128 | tf_op jit(solution)/shard_map/pallas_call | solution.py:82
  106.5 4.1 %shard_map.54 = (f32[1024,8192]{1,0:T(8,128)}, f32[1024,8192]{1,0:T(8,128)}, f32[8,128]{1,0:T(8,128)}) custom-call(bf16[1024,256]{1,0:T(8,128)(2,1)S(1)} %copy-done.2, f32[256,128]{1,0:T(8,128)S(1)} %get-tuple-element.24.shift_ref, bf16[64,4096]{1,0:T(8,128)(2,1)S(1)} %bitcast.22, ...), custom_call_target="tpu_custom_call", output_to_operand_aliasing={{0}: (10, {}), {1}: (11, {})} | custom-call | flops 1073741824 | bytes 8388608 | tf_op jit(solution)/shard_map/pallas_call | solution.py:82
  (22 shorter events, 0.3 us)
Async XLA Ops:
  3.5 36.2 %all-to-all-start = ((bf16[8,8,9344]{2,0,1:T(8,128)(2,1)}), bf16[8,8,9344]{2,0,1:T(8,128)(2,1)S(1)}, u32[]{:S(2)}, u32[]{:S(2)}) async-start(bf16[8,8,9344]{2,0,1:T(8,128)(2,1)} %bitcast.33), calls=%async_computation | async-start | bytes 2392064 | tf_op jit(solution)/shard_map/all_to_all | solution.py:176
  10.8 8.0 %collective-permute-start = (bf16[8,16384]{1,0:T(8,128)(2,1)}, bf16[8,16384]{1,0:T(8,128)(2,1)S(1)}, u32[]{:S(2)}, u32[]{:S(2)}) collective-permute-start(bf16[8,16384]{1,0:T(8,128)(2,1)} %get-tuple-element.21), channel_id=1, source_target_pairs={{0,16},{8,24},{16,0},{24,8},{1,17},{9,25},{17,1},{25,9},{2,18},{10... | collective-permute-start | bytes 786440 | tf_op jit(solution)/shard_map/ppermute | solution.py:150
  39.8 6.7 %collective-permute-start.1 = (bf16[64,1152]{1,0:T(8,128)(2,1)S(1)}, bf16[64,1152]{1,0:T(8,128)(2,1)S(1)}, u32[]{:S(2)}, u32[]{:S(2)}) collective-permute-start(bf16[64,1152]{1,0:T(8,128)(2,1)S(1)} %pad_maximum_fusion.4), channel_id=1, source_target_pairs={{0,16},{8,24},{16,0},{24,8},{1,17},{9,25},{17,1},{25,9},{2,18},{10... | collective-permute-start | bytes 442376 | tf_op jit(solution)/shard_map/ppermute | solution.py:150
  41.3 26.7 %all-to-all-start.2 = ((bf16[8,8,7168]{2,0,1:T(8,128)(2,1)}), bf16[8,8,7168]{2,0,1:T(8,128)(2,1)S(1)}, u32[]{:S(2)}, u32[]{:S(2)}) async-start(bf16[8,8,7168]{2,0,1:T(8,128)(2,1)} %bitcast.34), calls=%async_computation.2 | async-start | bytes 1835008 | tf_op jit(solution)/shard_map/all_to_all | solution.py:176
  46.0 22.0 %collective-permute-start.4 = (bf16[64,7168]{1,0:T(8,128)(2,1)}, bf16[64,7168]{1,0:T(8,128)(2,1)}, u32[]{:S(2)}, u32[]{:S(2)}) collective-permute-start(bf16[64,7168]{1,0:T(8,128)(2,1)} %slice.30.refs_0_.refs_4_), channel_id=1, source_target_pairs={{0,16},{8,24},{16,0},{24,8},{1,17},{9,25},{17,1},{25,9},{2,18},{10... | collective-permute-start | bytes 2752520 | tf_op jit(solution)/shard_map/ppermute | solution.py:150
  46.6 1.5 %collective-permute-start.2 = (bf16[128,640]{1,0:T(8,128)(2,1)S(1)}, bf16[128,640]{1,0:T(8,128)(2,1)S(1)}, u32[]{:S(2)}, u32[]{:S(2)}) collective-permute-start(bf16[128,640]{1,0:T(8,128)(2,1)S(1)} %pad_maximum_fusion.3), channel_id=1, source_target_pairs={{0,8},{8,0},{16,24},{24,16},{1,9},{9,1},{17,25},{25,17},{2,10},{10... | collective-permute-start | bytes 491528 | tf_op jit(solution)/shard_map/ppermute | solution.py:150
  48.2 14.0 %collective-permute-start.3 = (bf16[256,512]{1,0:T(8,128)(2,1)S(1)}, bf16[256,512]{1,0:T(8,128)(2,1)S(1)}, u32[]{:S(2)}, u32[]{:S(2)}) collective-permute-start(bf16[256,512]{1,0:T(8,128)(2,1)S(1)} %slice.32), channel_id=1, source_target_pairs={{0,1},{1,0},{2,3},{3,2},{4,5},{5,4},{6,7},{7,6},{8,9},{9,8},{10,11... | collective-permute-start | bytes 786440 | tf_op jit(solution)/shard_map/ppermute | solution.py:150
  50.3 24.2 %collective-permute-start.5 = (bf16[64,7168]{1,0:T(8,128)(2,1)}, bf16[64,7168]{1,0:T(8,128)(2,1)}, u32[]{:S(2)}, u32[]{:S(2)}) collective-permute-start(bf16[64,7168]{1,0:T(8,128)(2,1)} %slice.30.refs_0_.refs_4_), channel_id=1, source_target_pairs={{0,8},{8,0},{16,24},{24,16},{1,9},{9,1},{17,25},{25,17},{2,10},{10... | collective-permute-start | bytes 2752520 | tf_op jit(solution)/shard_map/ppermute | solution.py:150
  62.6 0.8 copy-start
  68.0 6.5 %collective-permute-start.6 = (bf16[64,7168]{1,0:T(8,128)(2,1)}, bf16[64,7168]{1,0:T(8,128)(2,1)}, u32[]{:S(2)}, u32[]{:S(2)}) collective-permute-start(bf16[64,7168]{1,0:T(8,128)(2,1)} %collective-permute-done.4.refs_1_.refs_5_), channel_id=1, source_target_pairs={{0,8},{8,0},{16,24},{24,16},{1,9},{9,1},{17,25},{25,17},{2,10},{10... | collective-permute-start | bytes 2752520 | tf_op jit(solution)/shard_map/ppermute | solution.py:150
  68.0 22.8 %collective-permute-start.8 = (bf16[64,7168]{1,0:T(8,128)(2,1)S(1)}, bf16[64,7168]{1,0:T(8,128)(2,1)S(1)}, u32[]{:S(2)}, u32[]{:S(2)}) collective-permute-start(bf16[64,7168]{1,0:T(8,128)(2,1)S(1)} %bitcast.26), channel_id=1, source_target_pairs={{0,16},{8,24},{16,0},{24,8},{1,17},{9,25},{17,1},{25,9},{2,18},{10... | collective-permute-start | bytes 2752520 | tf_op jit(solution)/shard_map/ppermute | solution.py:150
  68.6 22.7 %collective-permute-start.9 = (bf16[64,7168]{1,0:T(8,128)(2,1)S(1)}, bf16[64,7168]{1,0:T(8,128)(2,1)S(1)}, u32[]{:S(2)}, u32[]{:S(2)}) collective-permute-start(bf16[64,7168]{1,0:T(8,128)(2,1)S(1)} %bitcast.27), channel_id=1, source_target_pairs={{0,8},{8,0},{16,24},{24,16},{1,9},{9,1},{17,25},{25,17},{2,10},{10... | collective-permute-start | bytes 2752520 | tf_op jit(solution)/shard_map/ppermute | solution.py:150
  68.8 22.0 %all-to-all-start.1 = ((bf16[8,8,4096]{2,0,1:T(8,128)(2,1)}), bf16[8,8,4096]{2,0,1:T(8,128)(2,1)S(1)}, u32[]{:S(2)}, u32[]{:S(2)}) async-start(bf16[8,8,4096]{2,0,1:T(8,128)(2,1)} %pad_maximum_fusion), calls=%async_computation.1 | async-start | bytes 1048576 | tf_op jit(solution)/shard_map/all_to_all | solution.py:176
  74.5 1.0 copy-start.1
  90.8 3.4 %collective-permute-start.10 = (bf16[64,7168]{1,0:T(8,128)(2,1)S(1)}, bf16[64,7168]{1,0:T(8,128)(2,1)}, u32[]{:S(2)}, u32[]{:S(2)}) collective-permute-start(bf16[64,7168]{1,0:T(8,128)(2,1)S(1)} %collective-permute-done.8.refs_1_.refs_5_), channel_id=1, source_target_pairs={{0,8},{8,0},{16,24},{24,16},{1,9},{9,1},{17,25},{25,17},{2,10},{10... | collective-permute-start | bytes 2752520 | tf_op jit(solution)/shard_map/ppermute | solution.py:150
  90.8 15.7 %collective-permute-start.7 = (bf16[64,4096]{1,0:T(8,128)(2,1)S(1)}, bf16[64,4096]{1,0:T(8,128)(2,1)S(1)}, u32[]{:S(2)}, u32[]{:S(2)}) collective-permute-start(bf16[64,4096]{1,0:T(8,128)(2,1)S(1)} %bitcast.21), channel_id=1, source_target_pairs={{0,8},{8,0},{16,24},{24,16},{1,9},{9,1},{17,25},{25,17},{2,10},{10... | collective-permute-start | bytes 1572872 | tf_op jit(solution)/shard_map/ppermute | solution.py:150
  94.1 1.0 copy-start.2
